TPU v7x, 32 devices: a whole 2x2x4 slice. The times are simulated.
32 devices in a mesh: dp: 8 (over z, x), seq: 4 (over y, core).
Axes of the slice: x: 2, y: 2, z: 4, core: 2. Of those that a mesh axis runs over, the one named last changes fastest.
Arguments:
- hidden_in: bfloat16 [8, 1024, 2048], P('dp', 'seq'), may hold values from -6 to 6
- doc_lengths: int32 [8, 4], P('dp'), may hold values from 1 to 512, 1024 in all within a row
- norm1_gain: bfloat16 [2048], P(('dp', 'seq')), may hold values from 0.5 to 1.5
- w_qkv: bfloat16 [2048, 6144], P(('dp', 'seq')), may hold values from -0.125 to 0.125
- conv_weight: bfloat16 [4, 6144], P(None, ('dp', 'seq')), may hold values from -3 to 3
- w_beta: bfloat16 [2048, 16], P(('dp', 'seq')), may hold values from -0.125 to 0.125
- head_gain: bfloat16 [2048], P(('dp', 'seq')), may hold values from 0.5 to 1.5
- w_out: bfloat16 [2048, 2048], P(('dp', 'seq')), may hold values from -0.125 to 0.125
- norm2_gain: bfloat16 [2048], P(('dp', 'seq')), may hold values from 0.5 to 1.5
- w_gate_up: bfloat16 [2048, 2, 5632], P('dp', None, 'seq'), may hold values from -0.125 to 0.125
- w_down: bfloat16 [5632, 2048], P('seq', 'dp'), may hold values from -0.15625 to 0.15625
- cotangent: bfloat16 [8, 1024, 2048], P('dp', 'seq'), may hold values from -6 to 6
Outputs:
- out: bfloat16 [8, 1024, 2048], P('dp', 'seq')
- grad_x: float32 [8, 1024, 2048], P('dp', 'seq')
- grad_norm1_gain: float32 [2048], P(('dp', 'seq'))
- grad_w_qkv: float32 [2048, 6144], P(('dp', 'seq'))
- grad_conv_weight: float32 [4, 6144], P(None, ('dp', 'seq'))
- grad_w_beta: float32 [2048, 16], P(('dp', 'seq'))
- grad_head_gain: float32 [2048], P(('dp', 'seq'))
- grad_w_out: float32 [2048, 2048], P(('dp', 'seq'))
- grad_norm2_gain: float32 [2048], P(('dp', 'seq'))
- grad_w_gate_up: float32 [2048, 2, 5632], P('dp', None, 'seq')
- grad_w_down: float32 [5632, 2048], P('seq', 'dp')
Inputs may be any that keep to these rules, and one draw needn't show every extreme that they name: `doc_lengths`: each row's 4 lengths sum to 1024; in every row the longest is 512.
All inputs are finite; a program needn't handle non-finite values.
Results may differ from a plain program's by a relative error of at most 0.017.
Values may be sent and summed in bfloat16 or wider, within the bound.
No kernel may reach another device: no remote copies, remote signals or barrier semaphores. Data moves between devices by JAX's collectives and lax.ppermute only.
A program may use at most 448 MiB of HBM per device.

v0:
```python
import jax
import jax.numpy as jnp
from jax import lax
from jax.sharding import PartitionSpec as P

D = 2048
H = 16
HD = 128
KCONV = 4
SPAN = 64


HIGH = lax.Precision.HIGHEST
EPS = 1e-05
UNIT_EPS = 1e-06


def shifted(value, axis, by):
    peers = lax.axis_size(axis)
    pairs = [(i, i + by) for i in range(peers) if 0 <= i + by < peers]
    return lax.ppermute(value, axis, pairs)


def prefix_2(value, axis, join, neutral, backward):
    count = lax.axis_size(axis)
    place = lax.axis_index(axis)
    ahead = count - 1 - place if backward else place
    gathered = jax.tree.map(
        lambda a, kind: lax.all_gather(a.astype(kind), axis),
        value,
        jax.tree.map(lambda a: jnp.bfloat16 if a.dtype == jnp.float32 else a.dtype, value),
    )
    state = jax.tree.map(lambda a, e: jnp.zeros_like(a) + jnp.asarray(e, a.dtype), value, neutral)

    def one(step, state):
        source = count - 1 - step if backward else step
        return join(
            state,
            jax.tree.map(
                lambda a, own: lax.dynamic_index_in_dim(a, source, 0, False).astype(own.dtype),
                gathered,
                value,
            ),
        )

    return lax.fori_loop(0, ahead, one, state)


def unit_heads(values):
    shaped = values.reshape(values.shape[0], H, HD)
    return shaped * lax.rsqrt(jnp.sum(shaped * shaped, axis=-1, keepdims=True) + UNIT_EPS)


def matmul_heads(left, right):
    return jnp.einsum("hij,hjk->hik", left, right, precision=HIGH)


def join_forward(earlier, later):
    return (matmul_heads(earlier[0], later[0]), matmul_heads(earlier[1], later[0]) + later[1])


def join_backward(earlier, later):
    carried = jnp.einsum("hvk,hlk->hvl", earlier[1], later[0], precision=HIGH)
    return (matmul_heads(later[0], earlier[0]), later[1] + carried)


def norm_back(grad_out, scaled, stat, gain):
    weighted = grad_out * gain
    gain_grad = jnp.sum(grad_out * scaled, axis=0)
    input_grad = stat * (weighted - scaled * jnp.mean(weighted * scaled, axis=-1, keepdims=True))
    return (input_grad, gain_grad)


def body(
    hidden_in,
    doc_lengths,
    norm1_gain,
    w_qkv,
    conv_weight,
    w_beta,
    head_gain,
    w_out,
    norm2_gain,
    w_gate_up,
    w_down,
    cotangent,
):
    tokens = hidden_in.shape[1]
    rim_rows = KCONV - 1
    blocks = tokens // SPAN
    seq_place = lax.axis_index("seq")
    places = seq_place * tokens + jnp.arange(tokens, dtype=jnp.int32)
    doc_ends = jnp.cumsum(doc_lengths[0])
    starts = doc_ends - doc_lengths[0]
    starts_at = jnp.max(jnp.where(starts[None, :] <= places[:, None], starts[None, :], 0), axis=1)
    gain_one, mat_qkv, conv_taps, mat_beta, gain_head, mat_out, gain_two = (
        lax.all_gather(norm1_gain, ("dp", "seq"), axis=0, tiled=True),
        lax.all_gather(w_qkv, ("dp", "seq"), axis=0, tiled=True),
        lax.all_gather(conv_weight, ("dp", "seq"), axis=1, tiled=True),
        lax.all_gather(w_beta, ("dp", "seq"), axis=0, tiled=True),
        lax.all_gather(head_gain, ("dp", "seq"), axis=0, tiled=True),
        lax.all_gather(w_out, ("dp", "seq"), axis=0, tiled=True),
        lax.all_gather(norm2_gain, ("dp", "seq"), axis=0, tiled=True),
    )
    mat_gu, mat_down = (
        lax.all_gather(w_gate_up, "dp", axis=0, tiled=True),
        lax.all_gather(w_down, "dp", axis=1, tiled=True),
    )
    inside = jnp.stack([places - delay >= starts_at for delay in range(KCONV)]).astype(jnp.float32)[
        :, :, None
    ]
    block_starts = starts_at.reshape(blocks, SPAN)
    block_first = places.reshape(blocks, SPAN)[:, :1]
    same_doc = (block_starts[:, :, None] == block_starts[:, None, :]).astype(jnp.float32)[:, None]
    index_rows = jnp.arange(SPAN)
    strict_low = (index_rows[:, None] > index_rows[None, :]).astype(jnp.float32)
    with_diag = (index_rows[:, None] >= index_rows[None, :]).astype(jnp.float32)
    carry_in = (block_starts < block_first).astype(jnp.float32)[:, None, :, None]
    last_doc = (block_starts == block_starts[:, -1:]).astype(jnp.float32)[:, None, :, None]
    carry_last = carry_in[:, :, -1:, :]
    identity_c = jnp.eye(SPAN, dtype=jnp.float32)
    identity_k = jnp.eye(HD, dtype=jnp.float32)
    identity_h = jnp.broadcast_to(identity_k, (H, HD, HD))
    zeros_h = jnp.zeros((H, HD, HD), jnp.float32)

    def to_blocks(array):
        return array.reshape(blocks, SPAN, H, HD).transpose(0, 2, 1, 3)

    def activate(extended, beta_lin, taps):
        mixed_conv = inside[0] * taps[0] * extended[rim_rows:]
        for delay in range(1, KCONV):
            mixed_conv = (
                mixed_conv
                + inside[delay]
                * taps[delay]
                * extended[rim_rows - delay : rim_rows - delay + tokens]
            )
        acts = jax.nn.silu(mixed_conv)
        value_rows = acts[:, 2 * D :].reshape(tokens, H, HD)
        return (
            unit_heads(acts[:, :D]),
            unit_heads(acts[:, D : 2 * D]),
            value_rows,
            jax.nn.sigmoid(beta_lin),
        )

    def prepare(activated):
        query_rows, key_rows, value_rows, rates = activated
        query_blk = to_blocks(query_rows)
        key_blk = to_blocks(key_rows)
        value_blk = to_blocks(value_rows)
        rate_blk = rates.reshape(blocks, SPAN, H).transpose(0, 2, 1)
        gram = jnp.einsum("nhcd,nhed->nhce", key_blk, key_blk, precision=HIGH)
        system = identity_c + rate_blk[..., :, None] * gram * strict_low * same_doc
        right_side = jnp.concatenate(
            [rate_blk[..., None] * carry_in * key_blk, rate_blk[..., None] * value_blk], axis=-1
        )
        solved = lax.linalg.triangular_solve(
            system, right_side, left_side=True, lower=True, unit_diagonal=True
        )
        w_part = solved[..., :HD]
        u_part = solved[..., HD:]
        last_keys = key_blk * last_doc
        trans = carry_last * identity_k - jnp.einsum(
            "nhcd,nhce->nhde", w_part, last_keys, precision=HIGH
        )
        local = jnp.einsum("nhcv,nhck->nhvk", u_part, last_keys, precision=HIGH)
        attend = (
            jnp.einsum("nhcd,nhed->nhce", query_blk, key_blk, precision=HIGH) * with_diag * same_doc
        )
        return (query_blk, w_part, u_part, trans, local, attend)

    def chain(pieces):

        def chain_advance(carried, element):
            product, memory = carried
            return (
                (matmul_heads(product, element[0]), matmul_heads(memory, element[0]) + element[1]),
                None,
            )

        summary, _ = lax.scan(chain_advance, (identity_h, zeros_h), (pieces[3], pieces[4]))
        return summary

    def emit(pieces, start_state):

        def emit_advance(memory, element):
            query_blk, w_part, u_part, trans, local, attend, enter = element
            from_state = jnp.einsum("hcd,hvd->hcv", query_blk, memory, precision=HIGH) * enter
            corrected = u_part - jnp.einsum("hcd,hvd->hcv", w_part, memory, precision=HIGH)
            result = from_state + jnp.einsum("hce,hev->hcv", attend, corrected, precision=HIGH)
            return (matmul_heads(memory, trans) + local, result)

        _, results = lax.scan(emit_advance, start_state, pieces + (carry_in,))
        return results.transpose(0, 2, 1, 3).reshape(tokens, H, HD)

    resid = hidden_in[0].astype(jnp.float32)
    stat_one = lax.rsqrt(jnp.mean(resid * resid, axis=-1, keepdims=True) + EPS)
    scaled_one = resid * stat_one
    normed_low = (scaled_one * gain_one.astype(jnp.float32)).astype(jnp.bfloat16)
    linear = jnp.dot(normed_low, mat_qkv, preferred_element_type=jnp.float32).astype(jnp.bfloat16)
    beta_lin = jnp.dot(normed_low, mat_beta, preferred_element_type=jnp.float32)
    rim = shifted(linear[tokens - rim_rows :], "seq", 1)
    extended = jnp.concatenate([rim, linear], axis=0).astype(jnp.float32)
    activated, activate_back = jax.vjp(activate, extended, beta_lin, conv_taps.astype(jnp.float32))
    pieces, prepare_back = jax.vjp(prepare, activated)
    summary, chain_back = jax.vjp(chain, pieces)
    prefix = prefix_2(summary, "seq", join_forward, (identity_h, zeros_h), False)
    start_state = prefix[1]
    mixed, emit_back = jax.vjp(emit, pieces, start_state)
    head_stat = lax.rsqrt(jnp.mean(mixed * mixed, axis=-1, keepdims=True) + EPS)
    head_scaled = mixed * head_stat
    head_low = (
        (head_scaled * gain_head.astype(jnp.float32).reshape(H, HD))
        .reshape(tokens, D)
        .astype(jnp.bfloat16)
    )
    attn = jnp.dot(head_low, mat_out, preferred_element_type=jnp.float32)
    middle = resid + attn
    stat_two = lax.rsqrt(jnp.mean(middle * middle, axis=-1, keepdims=True) + EPS)
    scaled_two = middle * stat_two
    normed_two = (scaled_two * gain_two.astype(jnp.float32)).astype(jnp.bfloat16)
    gathered = lax.all_gather(normed_two, "seq", axis=0, tiled=True)
    f_slice = mat_down.shape[0]
    gate_up = jnp.dot(gathered, mat_gu.reshape(D, 2 * f_slice), preferred_element_type=jnp.float32)
    gate = gate_up[:, :f_slice]
    upper = gate_up[:, f_slice:]
    act_low = (gate * jax.nn.sigmoid(gate) * upper).astype(jnp.bfloat16)
    ffn_out = lax.psum_scatter(
        jnp.dot(act_low, mat_down, preferred_element_type=jnp.float32).astype(jnp.bfloat16),
        "seq",
        scatter_dimension=0,
        tiled=True,
    ).astype(jnp.float32)
    result = (middle + ffn_out).astype(jnp.bfloat16)
    gu_mat = mat_gu.reshape(D, 2 * f_slice)
    cot_rows = cotangent[0]
    cot_all = lax.all_gather(cot_rows, "seq", axis=0, tiled=True)
    down_grad = jnp.einsum("tf,td->fd", act_low, cot_all, preferred_element_type=jnp.float32)
    act_grad = jnp.einsum("td,fd->tf", cot_all, mat_down, preferred_element_type=jnp.float32)
    sig_gate = jax.nn.sigmoid(gate)
    gate_grad = act_grad * upper * sig_gate * (1.0 + gate * (1.0 - sig_gate))
    upper_grad = act_grad * gate * sig_gate
    gu_grad = jnp.concatenate([gate_grad, upper_grad], axis=1).astype(jnp.bfloat16)
    gu_weight_grad = jnp.einsum(
        "td,tk->dk", gathered, gu_grad, preferred_element_type=jnp.float32
    ).reshape(D, 2, f_slice)
    normed_two_grad = lax.psum_scatter(
        jnp.einsum("tk,dk->td", gu_grad, gu_mat, preferred_element_type=jnp.float32).astype(
            jnp.bfloat16
        ),
        "seq",
        scatter_dimension=0,
        tiled=True,
    ).astype(jnp.float32)
    middle_part, gain_two_grad = norm_back(
        normed_two_grad, scaled_two, stat_two, gain_two.astype(jnp.float32)
    )
    middle_grad = cot_rows.astype(jnp.float32) + middle_part
    attn_low = middle_grad.astype(jnp.bfloat16)
    head_grad = jnp.einsum("te,de->td", attn_low, mat_out, preferred_element_type=jnp.float32)
    gain_heads = gain_head.astype(jnp.float32).reshape(H, HD)
    mixed_grad, gain_head_grad = norm_back(
        head_grad.reshape(tokens, H, HD), head_scaled, head_stat, gain_heads
    )
    pieces_first, direct_grad = emit_back(mixed_grad)
    after = prefix_2((summary[0], direct_grad), "seq", join_backward, (identity_h, zeros_h), True)[
        1
    ]
    trans_grad = jnp.einsum("hvk,hvl->hkl", start_state, after, precision=HIGH)
    (pieces_second,) = chain_back((trans_grad, after))
    pieces_total = jax.tree.map(jnp.add, pieces_first, pieces_second)
    (act_grads,) = prepare_back(pieces_total)
    ext_grad, beta_grad, taps_grad = activate_back(act_grads)
    edge_grad = shifted(ext_grad[:rim_rows].astype(jnp.bfloat16), "seq", -1).astype(jnp.float32)
    linear_grad = (
        ext_grad[rim_rows:] + jnp.pad(edge_grad, ((tokens - rim_rows, 0), (0, 0)))
    ).astype(jnp.bfloat16)
    beta_low = beta_grad.astype(jnp.bfloat16)
    normed_grad = jnp.einsum("tk,dk->td", linear_grad, mat_qkv, preferred_element_type=jnp.float32)
    normed_grad = normed_grad + jnp.einsum(
        "th,dh->td", beta_low, mat_beta, preferred_element_type=jnp.float32
    )
    beta_weight_grad = jnp.einsum(
        "td,th->dh", normed_low, beta_low, preferred_element_type=jnp.float32
    )
    resid_part, gain_one_grad = norm_back(
        normed_grad, scaled_one, stat_one, gain_one.astype(jnp.float32)
    )
    input_grad = middle_grad + resid_part
    qkv_part = jnp.einsum("td,tk->dk", normed_low, linear_grad, preferred_element_type=jnp.float32)
    out_part = jnp.einsum("td,te->de", head_low, attn_low, preferred_element_type=jnp.float32)
    wide_grads = lax.psum_scatter(
        jnp.concatenate([qkv_part, out_part], axis=1),
        ("dp", "seq"),
        scatter_dimension=0,
        tiled=True,
    )
    small_grads = (
        lax.psum_scatter(gain_one_grad, ("dp", "seq"), scatter_dimension=0, tiled=True),
        lax.psum_scatter(taps_grad, ("dp", "seq"), scatter_dimension=1, tiled=True),
        lax.psum_scatter(beta_weight_grad, ("dp", "seq"), scatter_dimension=0, tiled=True),
        lax.psum_scatter(gain_head_grad.reshape(D), ("dp", "seq"), scatter_dimension=0, tiled=True),
        lax.psum_scatter(gain_two_grad, ("dp", "seq"), scatter_dimension=0, tiled=True),
    )
    ffn_grads = (
        lax.psum_scatter(
            gu_weight_grad.astype(jnp.bfloat16), "dp", scatter_dimension=0, tiled=True
        ).astype(jnp.float32),
        lax.psum_scatter(
            down_grad.astype(jnp.bfloat16), "dp", scatter_dimension=1, tiled=True
        ).astype(jnp.float32),
    )
    qkv_weight_grad = wide_grads[:, : 3 * D]
    out_weight_grad = wide_grads[:, 3 * D :]
    return (
        result[None],
        input_grad[None],
        small_grads[0],
        qkv_weight_grad,
        small_grads[1],
        small_grads[2],
        small_grads[3],
        out_weight_grad,
        small_grads[4],
        ffn_grads[0],
        ffn_grads[1],
    )


def solution(mesh):
    in_specs = (
        P("dp", "seq", None),
        P("dp", None),
        P(("dp", "seq")),
        P(("dp", "seq"), None),
        P(None, ("dp", "seq")),
        P(("dp", "seq"), None),
        P(("dp", "seq")),
        P(("dp", "seq"), None),
        P(("dp", "seq")),
        P("dp", None, "seq"),
        P("seq", "dp"),
        P("dp", "seq", None),
    )
    out_specs = (
        P("dp", "seq", None),
        P("dp", "seq", None),
        P(("dp", "seq")),
        P(("dp", "seq"), None),
        P(None, ("dp", "seq")),
        P(("dp", "seq"), None),
        P(("dp", "seq")),
        P(("dp", "seq"), None),
        P(("dp", "seq")),
        P("dp", None, "seq"),
        P("seq", "dp"),
    )
    return jax.shard_map(body, mesh=mesh, in_specs=in_specs, out_specs=out_specs, check_vma=False)
```

profile of v0, /device:TPU:0, one launch (start us, length us, event | category | flops | bytes accessed | tf_op | source)
XLA Modules:
  0.0 2781.8 jit_solution(7252092940195896830)
XLA Ops:
  12.4 43.3 %all-reduce.22 = (bf16[2048]{0:T(1024)(128)(2,1)S(1)}, bf16[2048]{0:T(1024)(128)(2,1)S(1)}, bf16[2048]{0:T(1024)(128)(2,1)S(1)}) all-reduce(bf16[2048]{0:T(1024)(128)(2,1)S(1)} %dynamic-update-slice.1, bf16[2048]{0:T(1024)(128)(2,1)S(1)} %dynamic-update-slice, ...), channel_id=1, replica_groups=mesh['dp'=8,'seq'=4] {'dp','seq'}, use_global_device_ids=true, to_apply=%add.15 | all-reduce | flops 6144 | bytes 24576
  55.7 41.3 %all-gather.5 = bf16[32,192,4]{1,2,0:T(4,128)(2,1)S(1)} all-gather(bf16[1,192,4]{1,2,0:T(4,128)(2,1)} %bitcast.619), channel_id=1, replica_groups=mesh['dp'=8,'seq'=4] {'dp','seq'}, dimensions={0}, use_global_device_ids=true | all-gather | bytes 50688 | tf_op jit(solution)/shard_map/all_gather | solution.py:99
  97.1 38.4 %all-gather.4 = bf16[32,64,16]{1,2,0:T(8,128)(2,1)S(1)} all-gather(bf16[1,64,16]{1,2,0:T(8,128)(2,1)} %bitcast.618), channel_id=1, replica_groups=mesh['dp'=8,'seq'=4] {'dp','seq'}, dimensions={0}, use_global_device_ids=true | all-gather | bytes 67584 | tf_op jit(solution)/shard_map/all_gather | solution.py:100
  137.9 33.2 %all-gather.16.cloned.1.call-done = bf16[2048,6144]{1,0:T(8,128)(2,1)} async-done(((bf16[64,6144]{1,0:T(8,128)(2,1)}), bf16[2048,6144]{1,0:T(8,128)(2,1)}) %all-gather.16.cloned.1.call-update) | async-done | bytes 25165840 | tf_op jit(solution)/shard_map/all_gather | solution.py:98
  210.6 316.0 %custom-call.7 = f32[4,16,1,64,64]{3,4,2,1,0:T(8,128)} custom-call(f32[4,16,1,64,64]{4,3,2,1,0:T(8,128)} %add_bitcast_fusion.2), custom_call_target="InvertDiagBlocksLowerTriangular" | custom-call | tf_op jit(solution)/shard_map/jvp()/triangular_solve | solution.py:158
  563.7 43.6 %while.110 = (s32[]{:T(128)}, f32[16,128,128]{1,2,0:T(8,128)}, f32[16,128,128]{1,2,0:T(8,128)}, f32[4,16,128,128]{2,3,1,0:T(8,128)}, f32[4,16,128,128]{2,3,1,0:T...) while((s32[]{:T(128)}, f32[16,128,128]{1,2,0:T(8,128)}, ...), condition=%wide.region_5.6_spmd.clone, body=%wide.region_4.5_spmd.clone.sunk | while | flops 806092800 | bytes 32507536 | solution.py:182
  633.2 24.8 all-gather.28.cloned.1.call-done
  662.5 48.1 %while.107 = (s32[]{:T(128)}, f32[16,128,128]{1,2,0:T(8,128)S(1)}, f32[4,16,64,128]{3,1,2,0:T(8,128)}, f32[4,16,128,128]{2,3,1,0:T(8,128)}, f32[4,16,64,128]{3,2...) while((s32[]{:T(128)}, f32[16,128,128]{1,2,0:T(8,128)S(1)}, ...), condition=%wide.region_10.11_spmd, body=%wide.region_9.10_spmd.sunk | while | flops 906625024 | bytes 16780184 | solution.py:194
  717.2 21.1 all-gather.18.cloned.1.call-done
  748.8 153.8 %all-gather.22.cloned.1.call-done = bf16[2048,2,1408]{2,1,0:T(2,128)(2,1)} async-done(((bf16[256,2,1408]{2,1,0:T(2,128)(2,1)}), bf16[2048,2,1408]{2,1,0:T(2,128)(2,1)}) %all-gather.22.cloned.1.call-update) | async-done | bytes 11534352 | tf_op jit(solution)/shard_map/all_gather | solution.py:106
  914.0 23.3 all-gather.20.cloned.1.call-done
  973.3 95.7 %all-gather.24.cloned.1.call-done = bf16[1408,2048]{1,0:T(8,128)(2,1)} async-done(((bf16[1408,256]{1,0:T(8,128)(2,1)}), bf16[1408,2048]{1,0:T(8,128)(2,1)}) %all-gather.24.cloned.1.call-update) | async-done | bytes 5767184 | tf_op jit(solution)/shard_map/all_gather | solution.py:107
  1117.4 29.4 %reduce-scatter.13.cloned.1.call-done = bf16[256,2048]{1,0:T(8,128)(2,1)} async-done(((bf16[1024,2048]{1,0:T(8,128)(2,1)}), bf16[256,2048]{1,0:T(8,128)(2,1)}) %reduce-scatter.13.cloned.1.call-update) | async-done | bytes 1048592 | tf_op jit(solution)/shard_map/reduce_scatter | solution.py:248
  1150.1 43.8 %reduce-scatter.11.cloned.1.call-done = bf16[256,2048]{1,0:T(8,128)(2,1)} async-done(((bf16[1024,2048]{1,0:T(8,128)(2,1)}), bf16[256,2048]{1,0:T(8,128)(2,1)}) %reduce-scatter.11.cloned.1.call-update) | async-done | bytes 1048592 | tf_op jit(solution)/shard_map/reduce_scatter | solution.py:229
  1225.0 104.1 %while.111 = (s32[]{:T(128)}, f32[16,128,128]{1,2,0:T(8,128)S(1)}, f32[4,16,64,128]{3,2,1,0:T(8,128)}, f32[4,16,64,128]{3,2,1,0:T(8,128)}, f32[4,16,64,128]{3,2,...) while((s32[]{:T(128)}, f32[16,128,128]{1,2,0:T(8,128)S(1)}, ...), condition=%wide.region_18.19_spmd.clone, body=%wide.region_17.18_spmd.clone.sunk | while | flops 1813774336 | bytes 40377340 | solution.py:194
  1360.3 22.6 convert_element_type.215
  1431.0 52.0 %while.109 = (s32[]{:T(128)}, f32[16,128,128]{1,2,0:T(8,128)}, f32[16,128,128]{1,2,0:T(8,128)S(1)}, f32[4,16,128,128]{3,2,1,0:T(8,128)}, f32[4,16,128,128]{2,3,1...) while((s32[]{:T(128)}, f32[16,128,128]{1,2,0:T(8,128)}, ...), condition=%wide.region_22.23_spmd, body=%wide.region_21.22_spmd.sunk | while | flops 1610874880 | bytes 40895680 | solution.py:182
  1608.0 23.3 fusion.188
  1631.3 44.2 %pad_maximum_fusion = f32[2048,8192]{1,0:T(8,128)} fusion(f32[2048,2048]{1,0:T(8,128)} %fusion.184, f32[2048,6144]{1,0:T(8,128)} %fusion.188), kind=kLoop, calls=%fused_computation.126 | loop fusion | flops 16777216 | bytes 134217728 | tf_op jit(solution)/shard_map/concatenate | solution.py:294
  1681.6 145.3 %all-reduce.25.cloned.1.call-done = bf16[2048,2,1408]{2,1,0:T(2,128)(2,1)} async-done(((bf16[2048,2,1408]{2,1,0:T(2,128)(2,1)}), bf16[2048,2,1408]{2,1,0:T(2,128)(2,1)}) %all-reduce.25.cloned.1.call-update) | async-done | bytes 11534352
  1846.8 39.7 %all-reduce.21 = (f32[2048]{0:T(1024)S(1)}, f32[2048]{0:T(1024)S(1)}, f32[2048]{0:T(1024)S(1)}) all-reduce(f32[2048]{0:T(1024)S(1)} %get-tuple-element.1126, f32[2048]{0:T(1024)S(1)} %copy-done.98, f32[2048]{0:T(1024)S(1)} %copy-done.97), channel_id=8, replica_groups=mesh['dp'=8,'seq'=4] {'dp','seq'}, use_global_device_ids=true, to_apply=%region_30.31.clone | all-reduce | flops 6144 | bytes 49152
  1891.7 41.6 %reduce-scatter.19.cloned.1.call-done = f32[192,4]{1,0:T(8,128)} async-done(((f32[6144,4]{1,0:T(8,128)}), f32[192,4]{1,0:T(8,128)}) %reduce-scatter.19.cloned.1.call-update) | async-done | bytes 3088
  1934.8 134.9 %reduce-scatter.21.cloned.1.call-done = f32[64,16]{1,0:T(8,128)} async-done(((f32[2048,16]{1,0:T(8,128)}), f32[64,16]{1,0:T(8,128)}) %reduce-scatter.21.cloned.1.call-update) | async-done | bytes 4112
  2071.1 699.2 %reduce-scatter.15.cloned.1.call-done = f32[64,8192]{1,0:T(8,128)} async-done(((f32[2048,8192]{1,0:T(8,128)}), f32[64,8192]{1,0:T(8,128)}) %reduce-scatter.15.cloned.1.call-update) | async-done | bytes 2097168 | tf_op jit(solution)/shard_map/reduce_scatter | solution.py:293
  (616 shorter events, 765.5 us)
Async XLA Ops:
  7.2 163.9 %all-gather.16.cloned.1.call-start = ((), (), s32[]{:S(2)}) async-start(), calls=%async_computation.6 | async-start | bytes 25952256 | tf_op jit(solution)/shard_map/all_gather | solution.py:98
  7.9 625.3 %all-gather.26.cloned.1.call-start = ((), (), s32[]{:S(2)}) async-start(), calls=%async_computation.15 | async-start | bytes 2621440 | tf_op jit(solution)/shard_map/all_gather | solution.py:29
  137.2 406.1 %copy-start.91 = (f32[4,64]{1,0:T(4,128)}, f32[4,64]{1,0:T(4,128)S(1)}, u32[]{:S(2)}) copy-start(f32[4,64]{1,0:T(4,128)S(1)} %get-tuple-element.1277) | copy-start | bytes 3076
  137.4 389.2 %copy-start.66 = (f32[4,16,64]{2,1,0:T(8,128)}, f32[4,16,64]{2,1,0:T(8,128)S(1)}, u32[]{:S(2)}) copy-start(f32[4,16,64]{2,1,0:T(8,128)S(1)} %broadcast_multiply_fusion.1) | copy-start | bytes 49156
  137.5 485.5 %copy-start.52 = (f32[4,64,64]{2,1,0:T(8,128)}, f32[4,64,64]{2,1,0:T(8,128)S(1)}, u32[]{:S(2)}) copy-start(f32[4,64,64]{2,1,0:T(8,128)S(1)} %compare_convert_fusion) | copy-start | bytes 196612
  184.5 3.1 collective-permute-start
  187.0 339.6 %copy-start.58 = (f32[4,64,16]{1,2,0:T(8,128)}, f32[4,64,16]{1,2,0:T(8,128)S(1)}, u32[]{:S(2)}) copy-start(f32[4,64,16]{1,2,0:T(8,128)S(1)} %copy.587) | copy-start | bytes 49156
  202.1 420.9 %copy-start.1 = (f32[32,8,16,128]{3,2,1,0:T(8,128)}, f32[32,8,16,128]{3,2,1,0:T(8,128)S(1)}, u32[]{:S(2)}) copy-start(f32[32,8,16,128]{3,2,1,0:T(8,128)S(1)} %copy.499) | copy-start | bytes 6291460
  202.9 420.1 %copy-start.54 = (f32[4,64,16]{1,2,0:T(8,128)}, f32[4,64,16]{1,2,0:T(8,128)S(1)}, u32[]{:S(2)}) copy-start(f32[4,64,16]{1,2,0:T(8,128)S(1)} %copy.366) | copy-start | bytes 49156
  609.6 48.3 %all-gather.28.cloned.1.call-start = ((), (), s32[]{:S(2)}) async-start(), calls=%async_computation.16 | async-start | bytes 2621440 | tf_op jit(solution)/shard_map/all_gather | solution.py:29
  611.1 127.2 %all-gather.18.cloned.1.call-start = ((), (), s32[]{:S(2)}) async-start(), calls=%async_computation.7 | async-start | bytes 8650752 | tf_op jit(solution)/shard_map/all_gather | solution.py:102
  611.7 290.9 %all-gather.22.cloned.1.call-start = ((), (), s32[]{:S(2)}) async-start(), calls=%async_computation.9 | async-start | bytes 12976128 | tf_op jit(solution)/shard_map/all_gather | solution.py:106
  612.3 325.0 %all-gather.20.cloned.1.call-start = ((), (), s32[]{:S(2)}) async-start(), calls=%async_computation.8 | async-start | bytes 5242880 | tf_op jit(solution)/shard_map/all_gather | solution.py:223
  747.0 226.3 %all-gather.30.cloned.1.call-start = ((), (), s32[]{:S(2)}) async-start(), calls=%async_computation.17 | async-start | bytes 5242880 | tf_op jit(solution)/shard_map/all_gather | solution.py:238
  747.8 321.2 %all-gather.24.cloned.1.call-start = ((), (), s32[]{:S(2)}) async-start(), calls=%async_computation.10 | async-start | bytes 6488064 | tf_op jit(solution)/shard_map/all_gather | solution.py:107
  748.5 398.3 %reduce-scatter.13.cloned.1.call-start = ((), (), s32[]{:S(2)}) async-start(), calls=%async_computation.12 | async-start | bytes 5242880 | tf_op jit(solution)/shard_map/reduce_scatter | solution.py:248
  1104.0 89.9 %reduce-scatter.11.cloned.1.call-start = ((), (), s32[]{:S(2)}) async-start(), calls=%async_computation.11 | async-start | bytes 5242880 | tf_op jit(solution)/shard_map/reduce_scatter | solution.py:229
  1115.5 289.7 %all-gather.32.cloned.1.call-start = ((), (), s32[]{:S(2)}) async-start(), calls=%async_computation.18 | async-start | bytes 2621440 | tf_op jit(solution)/shard_map/all_gather | solution.py:29
  1330.3 347.2 %reduce-scatter.17.cloned.1.call-start = ((), (), s32[]{:S(2)}) async-start(), calls=%async_computation.14 | async-start | bytes 6488064 | tf_op jit(solution)/shard_map/reduce_scatter | solution.py:310
  1341.1 485.8 %all-reduce.25.cloned.1.call-start = ((), (), s32[]{:S(2)}) async-start(), calls=%async_computation.21 | async-start | bytes 23068672
  1383.0 550.3 %reduce-scatter.19.cloned.1.call-start = ((), (), s32[]{:S(2)}) async-start(), calls=%async_computation.19 | async-start | bytes 3244032
  1601.3 6.6 collective-permute-start.1
  1605.0 464.7 %reduce-scatter.21.cloned.1.call-start = ((), (), s32[]{:S(2)}) async-start(), calls=%async_computation.20 | async-start | bytes 1081344
  1607.9 1162.4 %reduce-scatter.15.cloned.1.call-start = ((), (), s32[]{:S(2)}) async-start(), calls=%async_computation.13 | async-start | bytes 69206016 | tf_op jit(solution)/shard_map/reduce_scatter | solution.py:293
  (123 other events, 1601.0 us)
Sparse Core Ops, SparseCore 0:
  10.9 160.1 all-gather.15
  609.7 23.3 all-gather.25
  635.3 22.5 all-gather.27
  660.7 77.5 all-gather.17
  740.3 162.2 all-gather.21
  904.6 32.6 all-gather.19
  938.8 34.4 all-gather.29
  975.4 93.5 all-gather.23
  1104.1 42.6 reduce-scatter.12
  1149.4 44.4 reduce-scatter.10
  1330.4 22.5 all-gather.31
  1356.6 110.3 reduce-scatter.16
  1470.9 355.9 all-reduce.24
  1832.1 101.0 reduce-scatter.18
  1935.9 133.7 reduce-scatter.20
  2072.0 698.2 reduce-scatter.14
where the time goes:
time: 2790 us; the launch traced here: 2780 us
  waiting for transfers between devices  1470 us (53%)
  matrix products  479 us (17%)
  other arithmetic  463 us (17%)
  local copies, waits for them, and re-layouts  181 us (6%)
  blocking collectives  163 us (6%)
    reduce_scatter x1, waiting for transfers between devices, body(): lax.psum_scatter(jnp.concatenate([qkv_part, out_part], axis=1), ('dp', 's...  699 us
    unnamed x19, waiting for transfers between devices  325 us
    another operation x4, other arithmetic, prepare(): lax.linalg.triangular_solve(system, right_side, left_side=True, lower=Tru...  318 us
    all_gather x1, waiting for transfers between devices, body(): lax.all_gather(w_gate_up, 'dp', axis=0, tiled=True)  154 us
    dot_general x36, matrix products, matmul_heads(): return jnp.einsum('hij,hjk->hik', left, right, precision=HIGH)  107 us
    all_gather x1, waiting for transfers between devices, body(): lax.all_gather(w_down, 'dp', axis=1, tiled=True)  95.7 us
    unnamed x2, blocking collectives  82.9 us
    unnamed x249, local copies, waits for them, and re-layouts  59.9 us
  transfers between devices with their start and end apart: 18, of which 15 were waited for; matrix products, arithmetic and copies ran while one was open for 18% of the time, Pallas kernels for 0%

commit v1 on v0

v1 whole, which is shorter than its diff:
```python
import functools
import jax
import jax.numpy as jnp
from jax import lax
from jax.experimental import pallas as pl
from jax.experimental.pallas import tpu as pltpu
from jax.sharding import Mesh, PartitionSpec as P

KCONV = 4
HD = 128
EPS = 1e-05
UNIT_EPS = 1e-06
F32 = jnp.float32
BF16 = jnp.bfloat16


def mm(left, right, dim_left=1, dim_right=0):
    return lax.dot_general(
        left.astype(BF16),
        right.astype(BF16),
        (((dim_left,), (dim_right,)), ((), ())),
        preferred_element_type=F32,
    )


def split(value):
    high = value.astype(BF16)
    return high, (value - high.astype(F32)).astype(BF16)


def mm3(left, right):
    lh, ll = split(left)
    rh, rl = split(right)
    return mm(lh, rh) + (mm(lh, rl) + mm(ll, rh))


def iota(shape, dim):
    return lax.broadcasted_iota(jnp.int32, shape, dim)


def doc_start(starts, row, place):
    found = jnp.zeros_like(place)
    for j in range(starts.shape[1]):
        first = starts[row, j]
        found = jnp.maximum(found, jnp.where(first <= place, first, 0))
    return found


def scalar_start(starts, row, place):
    found = jnp.int32(0)
    for j in range(starts.shape[1]):
        first = starts[row, j]
        found = jnp.maximum(found, jnp.where(first <= place, first, 0))
    return found


def shift_down(cur, tail, by):
    if by == 0:
        return cur
    rolled = pltpu.roll(cur, by, 0)
    edge = pltpu.roll(tail, by, 0)
    top = jnp.where(iota(edge.shape, 0) < by, edge, rolled[:8])
    return jnp.concatenate([top, rolled[8:]], axis=0)


def shift_up(cur, head, by):
    if by == 0:
        return cur
    size = cur.shape[0]
    rolled = pltpu.roll(cur, size - by, 0)
    edge = pltpu.roll(head, 8 - by, 0)
    last = jnp.where(iota(edge.shape, 0) >= 8 - by, edge, rolled[size - 8 :])
    return jnp.concatenate([rolled[: size - 8], last], axis=0)


class Masks:
    def __init__(self, starts, row, base, size):
        place = base + iota((size, HD), 0)
        start = doc_start(starts, row, place)
        self.inside = [(place - i >= start).astype(F32) for i in range(KCONV)]
        self.carry_in = (start < base).astype(F32)
        last = scalar_start(starts, row, base + size - 1)
        self.last_doc = (start == last).astype(F32)
        self.carry_last = (last < base).astype(F32)
        rows, cols = iota((size, size), 0), iota((size, size), 1)
        start_row = doc_start(starts, row, base + rows)
        start_col = doc_start(starts, row, base + cols)
        same = start_row == start_col
        self.strict = (same & (rows > cols)).astype(F32)
        self.diag = (same & (rows >= cols)).astype(F32)
        self.diag_t = (same & (rows <= cols)).astype(F32)


def conv_of(cur, tail, taps, masks):
    shifted = [shift_down(cur, tail, i) * masks.inside[i] for i in range(KCONV)]
    total = shifted[0] * taps[0:1]
    for i in range(1, KCONV):
        total = total + shifted[i] * taps[i : i + 1]
    return shifted, total


def unit(values):
    return lax.rsqrt(jnp.sum(values * values, axis=-1, keepdims=True) + UNIT_EPS)


def inverse(lower, size):
    rows, cols = iota((size, size), 0), iota((size, size), 1)
    low = jnp.where((rows // 16) == (cols // 16), lower, 0.0)
    eye = (rows == cols).astype(F32)
    square = mm3(low, low)
    found = eye - low
    found = found + mm3(found, square)
    square = mm3(square, square)
    found = found + mm3(found, square)
    square = mm3(square, square)
    found = found + mm3(found, square)
    width = 16
    while width < size:
        cross = jnp.where(
            ((rows // (2 * width)) == (cols // (2 * width))) & ((rows // width) != (cols // width)),
            lower,
            0.0,
        )
        found = found - mm3(mm3(found, cross), found)
        width *= 2
    return found


def forward_kernel(heads, rows, size, starts, place, lin, taps, gain, low_out, mixed_out, inv_out, fix_out, err_out, mem_out, memory, tails):
    step = pl.program_id(0)
    base = step * size

    @pl.when(step == 0)
    def _():
        memory[...] = jnp.zeros_like(memory)
        tails[...] = jnp.zeros_like(tails)

    for row in range(rows):
        masks = Masks(starts, row, base, size)
        for head in range(heads):
            pair = row * heads + head

            def group(kind):
                at = (kind * heads + head) * HD
                cur = lin[0, 0, row, 0, :, at : at + HD].astype(BF16).astype(F32)
                tail = tails[row, :, at : at + HD]
                _, conv = conv_of(cur, tail, taps[:, at : at + HD], masks)
                tails[row, :, at : at + HD] = cur[size - 8 :]
                return conv * jax.nn.sigmoid(conv)

            query, key, value = group(0), group(1), group(2)
            query = query * unit(query)
            key = key * unit(key)
            at = 3 * heads * HD + head
            rate = jnp.broadcast_to(
                jax.nn.sigmoid(lin[0, 0, row, 0, :, at : at + 1]), (size, HD)
            )
            rate_sq = rate if size == HD else rate[:, :size]
            stacked = jnp.concatenate([query, key], axis=0)
            gram = mm(stacked, key, 1, 1)
            inv = inverse(rate_sq * gram[size:] * masks.strict, size)
            attend = gram[:size] * masks.diag
            state = memory[pair]
            read = mm(stacked, state)
            error = value - masks.carry_in * read[size:]
            fix = mm(inv, rate * error)
            mixed = masks.carry_in * read[:size] + mm(attend, fix)
            memory[pair] = masks.carry_last * state + mm(key * masks.last_doc, fix, 0, 0)
            stat = lax.rsqrt(jnp.mean(mixed * mixed, axis=-1, keepdims=True) + EPS)
            at = head * HD
            low_out[0, 0, row, 0, :, at : at + HD] = (mixed * stat * gain[:, at : at + HD]).astype(BF16)
            mixed_out[0, 0, row, 0, :, at : at + HD] = mixed
            inv_out[0, pair] = inv.astype(BF16)
            fix_out[0, pair] = fix
            err_out[0, pair] = error
            mem_out[0, pair] = state


def backward_kernel(heads, rows, size, steps, starts, place, lin, edge, taps, gain, mixed_in, grad_in, inv_in, fix_in, err_in, mem_in, dlin_out, dtaps_out, dgain_out, dmemory, nexts):
    step = pl.program_id(0)
    chunk = steps - 1 - step
    base = chunk * size

    @pl.when(step == 0)
    def _():
        dmemory[...] = jnp.zeros_like(dmemory)
        nexts[...] = jnp.zeros_like(nexts)
        dtaps_out[...] = jnp.zeros_like(dtaps_out)
        dgain_out[...] = jnp.zeros_like(dgain_out)

    lanes = iota((size, HD), 1)
    for row in range(rows):
        masks = Masks(starts, row, base, size)
        place_next = base + size + iota((8, HD), 0)
        start_next = doc_start(starts, row, place_next)
        inside_next = [(place_next - i >= start_next).astype(F32) for i in range(KCONV)]
        rate_grads = jnp.zeros((size, HD), F32)
        for head in range(heads):
            pair = row * heads + head

            def group(kind):
                at = (kind * heads + head) * HD
                cur = lin[0, 0, row, 0, :, at : at + HD].astype(BF16).astype(F32)
                tail = edge[0, 0, row, 0, :, at : at + HD].astype(BF16).astype(F32)
                shifted, conv = conv_of(cur, tail, taps[:, at : at + HD], masks)
                sig = jax.nn.sigmoid(conv)
                return shifted, conv * sig, sig * (1.0 + conv * (1.0 - sig))

            def group_back(kind, shifted, slope, grad):
                at = (kind * heads + head) * HD
                dconv = grad * slope
                after = nexts[row, :, at : at + HD]
                total = None
                for i in range(KCONV):
                    dtaps_out[i : i + 1, at : at + HD] += jnp.sum(shifted[i] * dconv, axis=0, keepdims=True)
                    back = shift_up(dconv * masks.inside[i], after * inside_next[i], i) * taps[i : i + 1, at : at + HD]
                    total = back if total is None else total + back
                nexts[row, :, at : at + HD] = dconv[:8]
                dlin_out[0, 0, row, 0, :, at : at + HD] = total.astype(BF16)

            q_shift, query, q_slope = group(0)
            k_shift, key, k_slope = group(1)
            v_shift, _, v_slope = group(2)
            q_unit, k_unit = unit(query), unit(key)
            query = query * q_unit
            key = key * k_unit
            at = 3 * heads * HD + head
            rate = jnp.broadcast_to(
                jax.nn.sigmoid(lin[0, 0, row, 0, :, at : at + 1]), (size, HD)
            )
            rate_sq = rate if size == HD else rate[:, :size]

            at = head * HD
            mixed = mixed_in[0, 0, row, 0, :, at : at + HD]
            dhead = grad_in[0, 0, row, 0, :, at : at + HD].astype(F32)
            stat = lax.rsqrt(jnp.mean(mixed * mixed, axis=-1, keepdims=True) + EPS)
            scaled = mixed * stat
            dgain_out[:, at : at + HD] += jnp.sum(dhead * scaled, axis=0, keepdims=True)
            weighted = dhead * gain[:, at : at + HD]
            dmixed = stat * (weighted - scaled * jnp.mean(weighted * scaled, axis=-1, keepdims=True))

            fix, error, state = fix_in[0, pair], err_in[0, pair], mem_in[0, pair]
            dstate = dmemory[pair]
            gram = mm(key, jnp.concatenate([key, query], axis=0), 1, 1)
            gram_kk = gram[:, :size]
            attend_t = gram[:, size:] * masks.diag_t
            dfix = mm(attend_t, dmixed) + mm(key * masks.last_doc, dstate)
            dright = mm(inv_in[0, pair], dfix, 0, 0)
            both = mm(jnp.concatenate([dmixed, -dright], axis=0), fix, 1, 1)
            dattend = both[:size] * masks.diag
            dlower = both[size:] * masks.strict
            dlower_gram = dlower * rate_sq
            drate = jnp.sum(dright * error, axis=-1, keepdims=True) + jnp.sum(
                dlower * gram_kk, axis=-1, keepdims=True
            )
            dread_q = masks.carry_in * dmixed
            dread_k = -(rate * masks.carry_in * dright)
            dread = jnp.concatenate([dread_q, dread_k], axis=0)
            stacked = jnp.concatenate([query, key], axis=0)
            from_state = mm(dread, state, 1, 1)
            dquery = from_state[:size] + mm(dattend, key)
            dkey = (
                from_state[size:]
                + mm(dattend, query, 0, 0)
                + mm(dlower_gram + dlower_gram.T, key)
                + masks.last_doc * mm(fix, dstate, 1, 1)
            )
            dmemory[pair] = masks.carry_last * dstate + mm(stacked, dread, 0, 0)
            dvalue = rate * dright
            dquery = q_unit * (dquery - query * jnp.sum(dquery * query, axis=-1, keepdims=True))
            dkey = k_unit * (dkey - key * jnp.sum(dkey * key, axis=-1, keepdims=True))
            group_back(0, q_shift, q_slope, dquery)
            group_back(1, k_shift, k_slope, dkey)
            group_back(2, v_shift, v_slope, dvalue)
            rate_grads = jnp.where(lanes == head, drate * rate * (1.0 - rate), rate_grads)
        at = 3 * heads * HD
        dlin_out[0, 0, row, 0, :, at : at + HD] = rate_grads.astype(BF16)


def blocks_of(array, tokens):
    return array.reshape(tokens + array.shape[1:])


def chunk_at(step, place):
    block = (step // 2) ^ place[0]
    return block % 2, step % 2, block // 2


def delta_forward(lin, taps, gain, starts, place, heads, layout):
    cores, halves, rows, folds, size = layout
    steps = cores * halves * folds
    pairs = rows * heads
    wide = lin.shape[1]

    def at_chunk(step, starts, place):
        core, half, fold = chunk_at(step, place)
        return core, half, 0, fold, 0, 0

    def token_block(columns):
        return pl.BlockSpec((1, 1, rows, 1, size, columns), at_chunk)

    def saved(columns, tall):
        return pl.BlockSpec((1, pairs, tall, columns), lambda step, starts, place: (step, 0, 0, 0))

    def tokens(columns, kind):
        return jax.ShapeDtypeStruct(layout + (columns,), kind)

    total = cores * halves * rows * folds * size
    outs = pl.pallas_call(
        functools.partial(forward_kernel, heads, rows, size),
        grid_spec=pltpu.PrefetchScalarGridSpec(
            num_scalar_prefetch=2,
            grid=(steps,),
            in_specs=[
                token_block(wide),
                pl.BlockSpec(taps.shape, lambda step, starts, place: (0, 0)),
                pl.BlockSpec(gain.shape, lambda step, starts, place: (0, 0)),
            ],
            out_specs=[
                token_block(heads * HD),
                token_block(heads * HD),
                saved(size, size),
                saved(HD, size),
                saved(HD, size),
                saved(HD, HD),
            ],
            scratch_shapes=[
                pltpu.VMEM((pairs, HD, HD), F32),
                pltpu.VMEM((rows, 8, 3 * heads * HD), F32),
            ],
        ),
        out_shape=[
            tokens(heads * HD, BF16),
            tokens(heads * HD, F32),
            jax.ShapeDtypeStruct((steps, pairs, size, size), BF16),
            jax.ShapeDtypeStruct((steps, pairs, size, HD), F32),
            jax.ShapeDtypeStruct((steps, pairs, size, HD), F32),
            jax.ShapeDtypeStruct((steps, pairs, HD, HD), F32),
        ],
        compiler_params=pltpu.CompilerParams(
            dimension_semantics=("arbitrary",), vmem_limit_bytes=40 * 1024 * 1024
        ),
        cost_estimate=pl.CostEstimate(
            flops=total * HD * HD * heads * 60, bytes_accessed=total * wide * 8, transcendentals=total * heads * HD * 3
        ),
        name="delta_forward",
    )(starts, place, lin.reshape(layout + (wide,)), taps, gain)
    low, mixed = outs[:2]
    return low.reshape(total, heads * HD), mixed, tuple(outs[2:])


def delta_backward(lin, taps, gain, starts, place, mixed, dhead, saves, heads, layout):
    cores, halves, rows, folds, size = layout
    steps = cores * halves * folds
    pairs = rows * heads
    wide = lin.shape[1]
    total = cores * halves * rows * folds * size

    def at_chunk(step, starts, place):
        core, half, fold = chunk_at(steps - 1 - step, place)
        return core, half, 0, fold, 0, 0

    def at_edge(step, starts, place):
        core, half, fold = chunk_at(jnp.maximum(steps - 2 - step, 0), place)
        return core, half, 0, fold, size // 8 - 1, 0

    def token_block(columns):
        return pl.BlockSpec((1, 1, rows, 1, size, columns), at_chunk)

    def saved(columns, tall):
        return pl.BlockSpec((1, pairs, tall, columns), lambda step, starts, place: (steps - 1 - step, 0, 0, 0))

    whole = lambda step, starts, place: (0, 0)
    lin_blocks = lin.reshape(layout + (wide,))
    dlin, dtaps, dgain = pl.pallas_call(
        functools.partial(backward_kernel, heads, rows, size, steps),
        grid_spec=pltpu.PrefetchScalarGridSpec(
            num_scalar_prefetch=2,
            grid=(steps,),
            in_specs=[
                token_block(wide),
                pl.BlockSpec((1, 1, rows, 1, 8, wide), at_edge),
                pl.BlockSpec(taps.shape, whole),
                pl.BlockSpec(gain.shape, whole),
                token_block(heads * HD),
                token_block(heads * HD),
                saved(size, size),
                saved(HD, size),
                saved(HD, size),
                saved(HD, HD),
            ],
            out_specs=[
                token_block(wide),
                pl.BlockSpec(taps.shape, whole),
                pl.BlockSpec(gain.shape, whole),
            ],
            scratch_shapes=[
                pltpu.VMEM((pairs, HD, HD), F32),
                pltpu.VMEM((rows, 8, 3 * heads * HD), F32),
            ],
        ),
        out_shape=[
            jax.ShapeDtypeStruct(layout + (wide,), BF16),
            jax.ShapeDtypeStruct(taps.shape, F32),
            jax.ShapeDtypeStruct(gain.shape, F32),
        ],
        compiler_params=pltpu.CompilerParams(
            dimension_semantics=("arbitrary",), vmem_limit_bytes=40 * 1024 * 1024
        ),
        cost_estimate=pl.CostEstimate(
            flops=total * HD * HD * heads * 60, bytes_accessed=total * wide * 10, transcendentals=total * heads * HD * 3
        ),
        name="delta_backward",
    )(starts, place, lin_blocks, lin_blocks, taps, gain, mixed, dhead.reshape(layout + (heads * HD,)), *saves)
    return dlin.reshape(total, wide), dtaps, dgain


def partner(value, axis, bit):
    count = lax.axis_size(axis)
    return lax.ppermute(value, axis, [(i, i ^ bit) for i in range(count)])


def gather_z(piece):
    return [piece] + [partner(piece, "z", k) for k in range(1, lax.axis_size("z"))]


def permute_z(array):
    rows, wide = array.shape
    count = lax.axis_size("z")
    place = lax.axis_index("z")
    blocks = [array[:, k * (wide // count) : (k + 1) * (wide // count)] for k in range(count)]
    bit = 1
    while bit < count:
        odd = (place & bit) != 0
        blocks = [jnp.where(odd, blocks[k ^ bit], blocks[k]) for k in range(count)]
        bit *= 2
    return jnp.concatenate(blocks, axis=1)


def steps_of(half):
    folds = lax.axis_size("s") // 2
    along_y = []
    bit = 2
    while bit < 2 * folds:
        along_y.append(("s", bit))
        bit *= 2
    return [("x", 1)] + along_y if half == 0 else along_y + [("x", 1)]


def axis_of(step):
    axis, bit = step
    return 0 if axis == "x" else 1


def gather_group(own):
    tokens, wide = own.shape
    folds = lax.axis_size("s") // 2
    halves = []
    for half in range(2):
        part = own[half * (tokens // 2) : (half + 1) * (tokens // 2)].reshape(1, 1, tokens // 2, wide)
        for step in steps_of(half):
            part = jnp.concatenate([part, partner(part, *step)], axis=axis_of(step))
        halves.append(part)
    mine = jnp.stack(halves)
    return mine, partner(mine, "s", 1)


def scatter_group(mine, theirs):
    _, _, folds, size, wide = mine.shape
    arrived = partner(theirs.astype(BF16), "s", 1)
    total = mine.astype(F32) + arrived.astype(F32)
    halves = []
    for half in range(2):
        part = total[half]
        for step in reversed(steps_of(half)):
            dim = axis_of(step)
            count = part.shape[dim] // 2
            keep = lax.slice_in_dim(part, 0, count, axis=dim)
            send = lax.slice_in_dim(part, count, 2 * count, axis=dim)
            part = keep + partner(send.astype(BF16), *step).astype(F32)
        halves.append(part.reshape(size, wide))
    return jnp.concatenate(halves, axis=0)


def norm_back(grad_out, scaled, stat, gain):
    weighted = grad_out * gain
    gain_grad = jnp.sum(grad_out * scaled, axis=0)
    input_grad = stat * (weighted - scaled * jnp.mean(weighted * scaled, axis=-1, keepdims=True))
    return (input_grad, gain_grad)


def dot(left, right, dim_left=1, dim_right=0):
    return lax.dot_general(left, right, (((dim_left,), (dim_right,)), ((), ())), preferred_element_type=F32)


def after(value, *others):
    return lax.optimization_barrier((value,) + others)[0]


def body(
    hidden_in,
    doc_lengths,
    norm1_gain,
    w_qkv,
    conv_weight,
    w_beta,
    head_gain,
    w_out,
    norm2_gain,
    w_gate_up,
    w_down,
    cotangent,
):
    deep, pair, seq = lax.axis_size("z"), lax.axis_size("x"), lax.axis_size("s")
    place_z, place_x, place_s = lax.axis_index("z"), lax.axis_index("x"), lax.axis_index("s")
    team = pair * seq
    devices = deep * team
    place = place_x * seq + place_s
    tokens, wide = hidden_in.shape[1:]
    folds, size = seq // 2, tokens // 2
    layout = (2, 2, pair, folds, size)
    rows_each = w_qkv.shape[0]
    total_heads = w_beta.shape[1]
    heads = total_heads // team
    span = heads * HD
    block = wide // deep
    taps_each = conv_weight.shape[1]

    small = jnp.concatenate(
        [
            norm1_gain,
            norm2_gain,
            head_gain,
            conv_weight.reshape(-1),
            w_beta.reshape(-1),
        ]
    )
    length = small.shape[0]
    padded = -(-length // 128) * 128
    small = jnp.pad(small, (0, padded - length))
    small = lax.all_to_all(
        jnp.broadcast_to(small[None], (devices, padded)), ("z", "x", "s"), 0, 0, tiled=True
    )
    gain_one = small[:, :rows_each].reshape(1, wide).astype(F32)
    gain_two = small[:, rows_each : 2 * rows_each].reshape(1, wide).astype(F32)
    gain_head = lax.dynamic_slice_in_dim(
        small[:, 2 * rows_each : 3 * rows_each].reshape(1, wide), place * span, span, axis=1
    ).astype(F32)
    at = 3 * rows_each
    taps = small[:, at : at + KCONV * taps_each].reshape(devices, KCONV, taps_each)
    taps = taps.transpose(1, 0, 2).reshape(KCONV, 3, team, span)
    taps = lax.dynamic_index_in_dim(taps, place, 2, False).reshape(KCONV, 3 * span).astype(F32)
    at = at + KCONV * taps_each
    betas = small[:, at:length].reshape(deep, team * rows_each, total_heads)
    betas = lax.dynamic_slice_in_dim(betas, place * heads, heads, axis=2)
    betas = lax.dynamic_index_in_dim(betas, place_z, 0, False)

    cut = w_qkv.reshape(rows_each, 3, team, span).transpose(2, 0, 1, 3).reshape(team, rows_each, 3 * span)
    cut = lax.all_to_all(cut, ("x", "s"), 0, 0, tiled=True).reshape(team * rows_each, 3 * span)
    cut = jnp.concatenate([cut, jnp.pad(betas, ((0, 0), (0, HD - heads)))], axis=1)
    qkv_pieces = gather_z(cut)
    mat_qkv = jnp.concatenate(qkv_pieces, axis=0)
    out_from = [(i, (i % deep) * team + i // deep) for i in range(devices)]
    out_piece = lax.ppermute(w_out, ("z", "x", "s"), out_from)
    out_pieces = gather_z(out_piece)

    def absolute_z(pieces):
        bit = 1
        while bit < deep:
            odd = (place_z & bit) != 0
            pieces = [jnp.where(odd, pieces[k ^ bit], pieces[k]) for k in range(deep)]
            bit *= 2
        return jnp.concatenate(pieces, axis=0)

    mat_out = absolute_z(out_pieces)

    units = w_gate_up.shape[2] // pair
    second = place_x == 1

    def swap_x(array, axis):
        low_part = lax.slice_in_dim(array, 0, units, axis=axis)
        high_part = lax.slice_in_dim(array, units, 2 * units, axis=axis)
        mine = jnp.where(second, high_part, low_part)
        theirs = partner(jnp.where(second, low_part, high_part), "x", 1)
        return jnp.where(second, theirs, mine), jnp.where(second, mine, theirs)

    gu_piece = jnp.concatenate(swap_x(w_gate_up.transpose(1, 0, 2), 2), axis=1)
    down_piece = jnp.concatenate(swap_x(w_down, 0), axis=1)
    gu_piece, down_piece = lax.optimization_barrier((gu_piece, down_piece, mat_qkv))[:2]
    mat_gu = jnp.concatenate(gather_z(gu_piece), axis=1)
    mat_down = jnp.concatenate(gather_z(down_piece), axis=1)
    mat_gate, mat_up = mat_gu[0], mat_gu[1]

    starts = jnp.sum(
        jnp.where(
            jnp.arange(doc_lengths.shape[1])[None, :] < jnp.arange(doc_lengths.shape[1])[:, None],
            doc_lengths[0][None, :],
            0,
        ),
        axis=1,
    )[None]
    starts = jnp.concatenate([starts, partner(starts, "x", 1)], axis=0)
    place_seq = place_s.reshape(1).astype(jnp.int32)

    resid = hidden_in[0].astype(F32)
    stat_one = lax.rsqrt(jnp.mean(resid * resid, axis=-1, keepdims=True) + EPS)
    scaled_one = resid * stat_one
    normed_one = jnp.concatenate(
        gather_group(permute_z((scaled_one * gain_one).astype(BF16))), axis=0
    ).reshape(-1, wide)
    linear = dot(normed_one, mat_qkv)
    head_low, mixed, saves = delta_forward(linear, taps, gain_head, starts, place_seq, heads, layout)
    half_rows = head_low.shape[0] // 2
    part_shape = (2, pair, folds, size, wide)
    attn = scatter_group(
        dot(head_low[:half_rows], mat_out).reshape(part_shape),
        dot(head_low[half_rows:], mat_out).reshape(part_shape),
    )
    middle = resid + attn
    stat_two = lax.rsqrt(jnp.mean(middle * middle, axis=-1, keepdims=True) + EPS)
    scaled_two = middle * stat_two

    normed_two = jnp.concatenate(
        gather_group(permute_z((scaled_two * gain_two).astype(BF16))), axis=0
    ).reshape(-1, wide)
    cot_rows = cotangent[0]
    cot_all = jnp.concatenate(gather_group(permute_z(cot_rows)), axis=0).reshape(-1, wide)
    gate = dot(normed_two, mat_gate)
    upper = dot(normed_two, mat_up)
    sig_gate = jax.nn.sigmoid(gate)
    act_low = (gate * sig_gate * upper).astype(BF16)
    ffn_out = scatter_group(
        dot(act_low[:half_rows], mat_down).reshape(part_shape),
        dot(act_low[half_rows:], mat_down).reshape(part_shape),
    )
    result = (middle + permute_z(ffn_out)).astype(BF16)

    act_grad = dot(cot_all, mat_down, 1, 1)
    gate_grad = (act_grad * upper * sig_gate * (1.0 + gate * (1.0 - sig_gate))).astype(BF16)
    upper_grad = (act_grad * gate * sig_gate).astype(BF16)

    def into_group(rows):
        return (dot(gate_grad[rows], mat_gate, 1, 1) + dot(upper_grad[rows], mat_up, 1, 1)).reshape(part_shape)

    normed_two_grad = permute_z(
        scatter_group(into_group(slice(0, half_rows)), into_group(slice(half_rows, None)))
    )

    def sum_z(of_block):
        total = None
        for k in reversed(range(deep)):
            part = of_block(k)
            if k:
                part = partner(part.astype(BF16), "z", k).astype(F32)
            total = part if total is None else total + part
        return total

    def columns(array, k):
        return array[:, k * block : (k + 1) * block]

    gu_sum = sum_z(
        lambda k: jnp.stack(
            [dot(columns(normed_two, k), gate_grad, 0, 0), dot(columns(normed_two, k), upper_grad, 0, 0)]
        )
    )
    down_sum = sum_z(lambda k: dot(act_low, columns(cot_all, k), 0, 0))

    def back_x(array, axis, join):
        half = array.shape[axis] // 2
        low_part = lax.slice_in_dim(array, 0, half, axis=axis)
        high_part = lax.slice_in_dim(array, half, 2 * half, axis=axis)
        mine = jnp.where(second, high_part, low_part)
        theirs = partner(jnp.where(second, low_part, high_part).astype(BF16), "x", 1).astype(F32)
        return jnp.concatenate(
            [jnp.where(second, theirs, mine), jnp.where(second, mine, theirs)], axis=join
        )

    gu_weight_grad = back_x(gu_sum, 1, 2).transpose(1, 0, 2)
    down_weight_grad = back_x(down_sum, 1, 0)

    middle_part, gain_two_grad = norm_back(normed_two_grad, scaled_two, stat_two, gain_two)
    middle_grad = cot_rows.astype(F32) + middle_part

    attn_low = jnp.concatenate(gather_group(middle_grad.astype(BF16)), axis=0).reshape(-1, wide)
    head_grad = dot(attn_low, mat_out, 1, 1)
    lin_grad, taps_grad, gain_head_grad = delta_backward(
        linear, taps, gain_head, starts, place_seq, mixed, head_grad, saves, heads, layout
    )
    qkv_sum = sum_z(lambda k: dot(columns(normed_one, k), lin_grad, 0, 0))
    out_part = dot(head_low, attn_low, 0, 0).reshape(deep, span // deep, wide)
    out_sum = sum_z(lambda k: lax.dynamic_index_in_dim(out_part, place_z ^ k, 0, False))
    out_weight_grad = lax.ppermute(
        out_sum.astype(BF16), ("z", "x", "s"), [(b, a) for a, b in out_from]
    ).astype(F32)
    qkv_back = lax.all_to_all(
        qkv_sum.astype(BF16).reshape(team, rows_each, 3 * span + HD), ("x", "s"), 0, 0, tiled=True
    ).astype(F32)
    qkv_weight_grad = (
        qkv_back[:, :, : 3 * span]
        .reshape(team, rows_each, 3, span)
        .transpose(1, 2, 0, 3)
        .reshape(rows_each, 3 * wide)
    )
    beta_weight_grad = (
        qkv_back[:, :, 3 * span : 3 * span + heads].transpose(1, 0, 2).reshape(rows_each, total_heads)
    )
    normed_grad = permute_z(
        scatter_group(
            dot(lin_grad[:half_rows], mat_qkv, 1, 1).reshape(part_shape),
            dot(lin_grad[half_rows:], mat_qkv, 1, 1).reshape(part_shape),
        )
    )
    resid_part, gain_one_grad = norm_back(normed_grad, scaled_one, stat_one, gain_one)
    input_grad = middle_grad + resid_part

    head_full = lax.dynamic_update_slice(jnp.zeros((1, wide), F32), gain_head_grad, (0, place * span))
    taps_full = lax.dynamic_update_slice(
        jnp.zeros((KCONV, 3, team, span), F32),
        taps_grad.reshape(KCONV, 3, 1, span),
        (0, 0, place, 0),
    )
    taps_full = taps_full.reshape(KCONV, devices, taps_each).transpose(1, 0, 2).reshape(devices, KCONV * taps_each)
    small_grads = jnp.concatenate(
        [
            gain_one_grad.reshape(devices, rows_each),
            gain_two_grad.reshape(devices, rows_each),
            head_full.reshape(devices, rows_each),
            taps_full,
        ],
        axis=1,
    )
    length = small_grads.shape[1]
    small_grads = jnp.pad(small_grads, ((0, 0), (0, -length % 128)))
    small_grads = jnp.sum(
        lax.all_to_all(small_grads, ("z", "x", "s"), 0, 0, tiled=True), axis=0
    )
    return (
        result[None],
        input_grad[None],
        small_grads[:rows_each],
        qkv_weight_grad,
        small_grads[3 * rows_each : length].reshape(KCONV, taps_each),
        beta_weight_grad,
        small_grads[2 * rows_each : 3 * rows_each],
        out_weight_grad,
        small_grads[rows_each : 2 * rows_each],
        gu_weight_grad,
        down_weight_grad,
    )


def solution(mesh):
    outer, seq = mesh.shape["dp"], mesh.shape["seq"]
    grid = Mesh(mesh.devices.reshape(outer // 2, 2, seq), ("z", "x", "s"))
    every = ("z", "x", "s")
    rows = ("z", "x")
    in_specs = (
        P(rows, "s", None),
        P(rows, None),
        P(every),
        P(every, None),
        P(None, every),
        P(every, None),
        P(every),
        P(every, None),
        P(every),
        P(rows, None, "s"),
        P("s", rows),
        P(rows, "s", None),
    )
    out_specs = (
        P(rows, "s", None),
        P(rows, "s", None),
        P(every),
        P(every, None),
        P(None, every),
        P(every, None),
        P(every),
        P(every, None),
        P(every),
        P(rows, None, "s"),
        P("s", rows),
    )
    return jax.shard_map(body, mesh=grid, in_specs=in_specs, out_specs=out_specs, check_vma=False)
```

time: 2790 us -> 1170 us (0.42)
  waiting for transfers between devices: 1470 us -> 562 us
  other arithmetic: 463 us -> 99.3 us
  matrix products: 479 us -> 148 us
  blocking collectives: 163 us -> 0 us
  starting transfers between devices: 5.72 us -> 163 us
  Pallas kernels: 0 us -> 103 us
  local copies, waits for them, and re-layouts: 181 us -> 83 us
    reduce_scatter x4 -> x0, waiting for transfers between devices: 772 us -> none  [the longest x1 699 us: body(): lax.psum_scatter(jnp.concatenate([qkv_part, out_part], axis=1), ('dp', 's...]
    ppermute x2 -> x71, waiting for transfers between devices: 0.63 us -> 555 us  [the longest x69 555 us: partner(): return lax.ppermute(value, axis, [(i, i ^ bit) for i in range(count)])]
    all_gather x9 -> x0, waiting for transfers between devices: 374 us -> none  [the longest x1 154 us: body(): lax.all_gather(w_gate_up, 'dp', axis=0, tiled=True)]
    unnamed x19 -> x0, waiting for transfers between devices: 325 us -> none
    dot_general x103 -> x32, matrix products: 464 us -> 148 us  [dot(): lax.dot_general(left, right, (((dim_left,), (dim_right,)), ((), ())), pre...]
    another operation x6 -> x15, other arithmetic: 319 us -> 17.3 us  [the longest x12 13.7 us: gather_group(): mine = jnp.stack(halves)]
    ppermute x2 -> x71, starting transfers between devices: 3.65 us -> 146 us  [the longest x69 139 us: partner(): return lax.ppermute(value, axis, [(i, i ^ bit) for i in range(count)])]
    pallas_call x0 -> x2, Pallas kernels: none -> 103 us  [the longest x1 70.6 us: delta_forward(): pl.pallas_call(functools.partial(forward_kernel, heads, rows, size), grid...]
  transfers between devices with their start and end apart: 18 -> 75, of which waited for: 15 -> 35; matrix products, arithmetic and copies ran while one was open for 18% -> 19% of each run, Pallas kernels for 0% -> 3%
where the time goes in v1:
time: 1170 us; the launch traced here: 1160 us
  waiting for transfers between devices  562 us (48%)
  starting transfers between devices  163 us (14%)
  matrix products  148 us (13%)
  Pallas kernels  103 us (9%)
  other arithmetic  99.3 us (8%)
  local copies, waits for them, and re-layouts  83 us (7%)
    ppermute x69, waiting for transfers between devices, partner(): return lax.ppermute(value, axis, [(i, i ^ bit) for i in range(count)])  555 us
    dot_general x32, matrix products, dot(): lax.dot_general(left, right, (((dim_left,), (dim_right,)), ((), ())), pre...  148 us
    ppermute x69, starting transfers between devices, partner(): return lax.ppermute(value, axis, [(i, i ^ bit) for i in range(count)])  139 us
    pallas_call x1, Pallas kernels, delta_forward(): pl.pallas_call(functools.partial(forward_kernel, heads, rows, size), grid...  70.6 us
    unnamed x279, local copies, waits for them, and re-layouts  50.2 us
    pallas_call x1, Pallas kernels, delta_backward(): pl.pallas_call(functools.partial(backward_kernel, heads, rows, size, step...  32.1 us
  transfers between devices with their start and end apart: 75, of which 35 were waited for; matrix products, arithmetic and copies ran while one was open for 19% of the time, Pallas kernels for 3%

profile of v1, /device:TPU:0, one launch (start us, length us, event | category | flops | bytes accessed | tf_op | source)
XLA Modules:
  0.0 1161.7 jit_solution(1457613863087353243)
XLA Ops:
  25.5 12.6 %collective-permute-done.1 = bf16[1,1,128,2048]{3,2,1,0:T(8,128)(2,1)S(1)} collective-permute-done((bf16[1,1,128,2048]{3,2,1,0:T(8,128)(2,1)S(1)}, bf16[1,1,128,2048]{3,2,1,0:T(8,128)(2,1)S(1)}, u32[]{:S(2)}, u32[]{:S(2)}) %collective-permute-start.1) | collective-permute-done | bytes 524320 | tf_op jit(solution)/shard_map/ppermute | solution.py:420
  40.0 22.7 %collective-permute-done.2 = bf16[2,1,128,2048]{3,2,1,0:T(8,128)(2,1)S(1)} collective-permute-done((bf16[2,1,128,2048]{3,2,1,0:T(8,128)(2,1)S(1)}, bf16[2,1,128,2048]{3,2,1,0:T(8,128)(2,1)S(1)}, u32[]{:S(2)}, u32[]{:S(2)}) %collective-permute-start.2) | collective-permute-done | bytes 1048608 | tf_op jit(solution)/shard_map/ppermute | solution.py:420
  76.1 15.1 %collective-permute-done = s32[1,4]{1,0:T(1,128)S(1)} collective-permute-done((s32[1,4]{1,0:T(1,128)S(1)}, s32[1,4]{1,0:T(1,128)S(1)}, u32[]{:S(2)}, u32[]{:S(2)}) %collective-permute-start) | collective-permute-done | bytes 48 | tf_op jit(solution)/shard_map/ppermute | solution.py:420
  121.7 28.1 %collective-permute-done.6 = bf16[512,896]{1,0:T(8,128)(2,1)S(1)} collective-permute-done((bf16[512,896]{1,0:T(8,128)(2,1)S(1)}, bf16[512,896]{1,0:T(8,128)(2,1)S(1)}, u32[]{:S(2)}, u32[]{:S(2)}) %collective-permute-start.6) | collective-permute-done | bytes 917536 | tf_op jit(solution)/shard_map/ppermute | solution.py:420
  149.8 24.6 %collective-permute-done.7 = bf16[512,896]{1,0:T(8,128)(2,1)S(1)} collective-permute-done((bf16[512,896]{1,0:T(8,128)(2,1)S(1)}, bf16[512,896]{1,0:T(8,128)(2,1)S(1)}, u32[]{:S(2)}, u32[]{:S(2)}) %collective-permute-start.7) | collective-permute-done | bytes 917536 | tf_op jit(solution)/shard_map/ppermute | solution.py:420
  174.4 10.9 fusion.lin.edge
  185.3 70.6 %delta_forward.1 = (bf16[2,2,2,2,128,256]{5,4,3,2,1,0:T(8,128)(2,1)S(1)}, f32[2,2,2,2,128,256]{5,4,3,2,1,0:T(8,128)S(1)}, bf16[8,4,128,128]{3,2,1,0:T(8,128)(2,1...) custom-call(s32[2,4]{1,0:T(2,128)S(1)} %pad_add_fusion.starts, ...), custom_call_target="tpu_custom_call" | custom-call | flops 4026531840 | bytes 14680064 | tf_op jit(solution)/shard_map/delta_forward/pallas_call | solution.py:309
  290.0 18.9 %collective-permute-done.37 = bf16[2,1,128,2048]{3,2,1,0:T(8,128)(2,1)S(1)} collective-permute-done((bf16[2,1,128,2048]{3,2,1,0:T(8,128)(2,1)S(1)}, bf16[2,1,128,2048]{3,2,1,0:T(8,128)(2,1)S(1)}, u32[]{:S(2)}, u32[]{:S(2)}) %collective-permute-start.37) | collective-permute-done | bytes 1048608 | tf_op jit(solution)/shard_map/ppermute | solution.py:420
  310.3 20.4 %collective-permute-done.14 = bf16[2,1,128,2048]{3,2,1,0:T(8,128)(2,1)S(1)} collective-permute-done((bf16[2,1,128,2048]{3,2,1,0:T(8,128)(2,1)S(1)}, bf16[2,1,128,2048]{3,2,1,0:T(8,128)(2,1)S(1)}, u32[]{:S(2)}, u32[]{:S(2)}) %collective-permute-start.14) | collective-permute-done | bytes 1048608 | tf_op jit(solution)/shard_map/ppermute | solution.py:420
  378.5 19.5 %collective-permute-start.28 = (bf16[704,512]{1,0:T(8,128)(2,1)S(1)}, bf16[704,512]{1,0:T(8,128)(2,1)S(1)}, u32[]{:S(2)}, u32[]{:S(2)}) collective-permute-start(bf16[704,512]{1,0:T(8,128)(2,1)S(1)} %pad_maximum_fusion.29), channel_id=1, source_target_pairs={{0,8},{8,0},{16,24},{24,16},{1,9},{9,1},{17,25},{25,17},{2,10},{10... | collective-permute-start | bytes 2162696 | tf_op jit(solution)/shard_map/ppermute | solution.py:420
  400.6 15.7 %collective-permute-start.25 = (bf16[2,512,704]{1,2,0:T(8,128)(2,1)}, bf16[2,512,704]{1,2,0:T(8,128)(2,1)}, u32[]{:S(2)}, u32[]{:S(2)}) collective-permute-start(bf16[2,512,704]{1,2,0:T(8,128)(2,1)} %pad_maximum_fusion.11), channel_id=1, source_target_pairs={{0,8},{8,0},{16,24},{24,16},{1,9},{9,1},{17,25},{25,17},{2,10},{10... | collective-permute-start | bytes 4325384 | tf_op jit(solution)/shard_map/ppermute | solution.py:420
  416.6 13.3 %collective-permute-done.28 = bf16[704,512]{1,0:T(8,128)(2,1)S(1)} collective-permute-done((bf16[704,512]{1,0:T(8,128)(2,1)S(1)}, bf16[704,512]{1,0:T(8,128)(2,1)S(1)}, u32[]{:S(2)}, u32[]{:S(2)}) %collective-permute-start.28) | collective-permute-done | bytes 720928 | tf_op jit(solution)/shard_map/ppermute | solution.py:420
  433.0 15.9 %collective-permute-done.29 = bf16[704,512]{1,0:T(8,128)(2,1)S(1)} collective-permute-done((bf16[704,512]{1,0:T(8,128)(2,1)S(1)}, bf16[704,512]{1,0:T(8,128)(2,1)S(1)}, u32[]{:S(2)}, u32[]{:S(2)}) %collective-permute-start.29) | collective-permute-done | bytes 720928 | tf_op jit(solution)/shard_map/ppermute | solution.py:420
  455.8 32.0 %collective-permute-done.25 = bf16[2,512,704]{1,2,0:T(8,128)(2,1)} collective-permute-done((bf16[2,512,704]{1,2,0:T(8,128)(2,1)}, bf16[2,512,704]{1,2,0:T(8,128)(2,1)}, u32[]{:S(2)}, u32[]{:S(2)}) %collective-permute-start.25) | collective-permute-done | bytes 1441824 | tf_op jit(solution)/shard_map/ppermute | solution.py:420
  489.3 67.9 %collective-permute-done.26 = bf16[2,512,704]{1,2,0:T(8,128)(2,1)} collective-permute-done((bf16[2,512,704]{1,2,0:T(8,128)(2,1)}, bf16[2,512,704]{1,2,0:T(8,128)(2,1)}, u32[]{:S(2)}, u32[]{:S(2)}) %collective-permute-start.26) | collective-permute-done | bytes 1441824 | tf_op jit(solution)/shard_map/ppermute | solution.py:420
  590.9 14.0 %multiply_convert_fusion.1 = (bf16[2048,704]{0,1:T(8,128)(2,1)S(1)}, bf16[2048,704]{0,1:T(8,128)(2,1)}, bf16[2048,704]{0,1:T(8,128)(2,1)}) fusion(f32[2048,704]{0,1:T(8,128)} %fusion.184, f32[2048,704]{0,1:T(8,128)} %fusion.13, bf16[2048,2048]{1,0:T(8,128)(2,1)S(1)} %bitcast.309, bf16[2,2048,704]{1,2,0:T(8,128)(2,1)} %copy-done.95), kind=kOutput, calls=%fused_computation.10 | convolution fusion | flops 5928648704 | bytes 31457280 | tf_op jit(solution)/shard_map/dot_general | solution.py:493
  631.3 26.4 %collective-permute-start.68 = (bf16[704,512]{1,0:T(8,128)(2,1)}, bf16[704,512]{1,0:T(8,128)(2,1)}, u32[]{:S(2)}, u32[]{:S(2)}) collective-permute-start(bf16[704,512]{1,0:T(8,128)(2,1)} %fusion.109), channel_id=1, source_target_pairs={{0,16},{8,24},{16,0},{24,8},{1,17},{9,25},{17,1},{25,9},{2,18},{10... | collective-permute-start | bytes 2162696 | tf_op jit(solution)/shard_map/ppermute | solution.py:420
  708.3 17.0 %collective-permute-done.42 = bf16[2,1,128,2048]{3,2,1,0:T(8,128)(2,1)S(1)} collective-permute-done((bf16[2,1,128,2048]{3,2,1,0:T(8,128)(2,1)S(1)}, bf16[2,1,128,2048]{3,2,1,0:T(8,128)(2,1)S(1)}, u32[]{:S(2)}, u32[]{:S(2)}) %collective-permute-start.42) | collective-permute-done | bytes 1048608 | tf_op jit(solution)/shard_map/ppermute | solution.py:420
  754.8 17.1 %collective-permute-done.70 = bf16[704,256]{1,0:T(8,128)(2,1)S(1)} collective-permute-done((bf16[704,256]{1,0:T(8,128)(2,1)S(1)}, bf16[704,256]{1,0:T(8,128)(2,1)S(1)}, u32[]{:S(2)}, u32[]{:S(2)}) %collective-permute-start.70) | collective-permute-done | bytes 360480 | tf_op jit(solution)/shard_map/ppermute | solution.py:420
  788.6 64.3 %collective-permute-done.64 = bf16[2,512,704]{1,2,0:T(8,128)(2,1)} collective-permute-done((bf16[2,512,704]{1,2,0:T(8,128)(2,1)}, bf16[2,512,704]{1,2,0:T(8,128)(2,1)}, u32[]{:S(2)}, u32[]{:S(2)}) %collective-permute-start.64) | collective-permute-done | bytes 1441824 | tf_op jit(solution)/shard_map/ppermute | solution.py:420
  914.5 32.1 %delta_backward.1 = (bf16[2,2,2,2,128,896]{5,4,3,2,1,0:T(8,128)(2,1)}, f32[4,768]{1,0:T(4,128)S(1)}, f32[1,256]{1,0:T(1,128)S(1)}) custom-call(s32[2,4]{1,0:T(2,128)S(1)} %pad_add_fusion.starts, s32[1]{0:T(128)} %bitcast.2.place, f32[2,2,2,2,128,896]{5,4,3,2,1,0:T(8,128)} %fusion.lin.edge, f32[2,2,2,2,128,896]{5,4,3,2,1,0:T(8,128)} %fusion.lin.edge, ...), custom_call_target="tpu_custom_call" | custom-call | flops 4026531840 | bytes 18350080 | tf_op jit(solution)/shard_map/delta_backward/pallas_call | solution.py:375
  978.4 44.6 %collective-permute-done.60 = bf16[64,2048]{1,0:T(8,128)(2,1)S(1)} collective-permute-done((bf16[64,2048]{1,0:T(8,128)(2,1)S(1)}, bf16[64,2048]{1,0:T(8,128)(2,1)S(1)}, u32[]{:S(2)}, u32[]{:S(2)}) %collective-permute-start.60) | collective-permute-done | bytes 262176 | tf_op jit(solution)/shard_map/ppermute | solution.py:420
  1031.4 36.7 %collective-permute-done.57 = bf16[512,896]{1,0:T(8,128)(2,1)S(1)} collective-permute-done((bf16[512,896]{1,0:T(8,128)(2,1)S(1)}, bf16[512,896]{1,0:T(8,128)(2,1)S(1)}, u32[]{:S(2)}, u32[]{:S(2)}) %collective-permute-start.57) | collective-permute-done | bytes 917536 | tf_op jit(solution)/shard_map/ppermute | solution.py:420
  1106.9 14.8 %collective-permute-done.52 = bf16[2,1,128,2048]{3,2,1,0:T(8,128)(2,1)} collective-permute-done((bf16[2,1,128,2048]{3,2,1,0:T(8,128)(2,1)}, bf16[2,1,128,2048]{3,2,1,0:T(8,128)(2,1)}, u32[]{:S(2)}, u32[]{:S(2)}) %collective-permute-start.52) | collective-permute-done | bytes 1048608 | tf_op jit(solution)/shard_map/ppermute | solution.py:420
  (607 shorter events, 503.5 us)
Async XLA Ops:
  103.2 71.2 %collective-permute-start.7 = (bf16[512,896]{1,0:T(8,128)(2,1)S(1)}, bf16[512,896]{1,0:T(8,128)(2,1)S(1)}, u32[]{:S(2)}, u32[]{:S(2)}) collective-permute-start(bf16[512,896]{1,0:T(8,128)(2,1)S(1)} %pad_maximum_fusion.28), channel_id=1, source_target_pairs={{0,16},{8,24},{16,0},{24,8},{1,17},{9,25},{17,1},{25,9},{2,18},{10... | collective-permute-start | bytes 2752520 | tf_op jit(solution)/shard_map/ppermute | solution.py:420
  115.6 58.8 %collective-permute-start.8 = (bf16[512,896]{1,0:T(8,128)(2,1)S(1)}, bf16[512,896]{1,0:T(8,128)(2,1)S(1)}, u32[]{:S(2)}, u32[]{:S(2)}) collective-permute-start(bf16[512,896]{1,0:T(8,128)(2,1)S(1)} %pad_maximum_fusion.28), channel_id=1, source_target_pairs={{0,24},{8,16},{16,8},{24,0},{1,25},{9,17},{17,9},{25,1},{2,26},{10... | collective-permute-start | bytes 2752520 | tf_op jit(solution)/shard_map/ppermute | solution.py:420
  271.5 104.3 %collective-permute-start.23 = (bf16[2,256,704]{1,2,0:T(8,128)(2,1)}, bf16[2,256,704]{1,2,0:T(8,128)(2,1)}, u32[]{:S(2)}, u32[]{:S(2)}) collective-permute-start(bf16[2,256,704]{1,2,0:T(8,128)(2,1)} %broadcast_select_fusion.3), channel_id=1, source_target_pairs={{0,4},{4,0},{1,5},{5,1},{2,6},{6,2},{3,7},{7,3},{8,12},{12,8},{9,1... | collective-permute-start | bytes 2162696 | tf_op jit(solution)/shard_map/ppermute | solution.py:420
  357.2 205.9 %collective-permute-start.40 = (bf16[2,2,2,128,2048]{4,3,2,1,0:T(8,128)(2,1)}, bf16[2,2,2,128,2048]{4,3,2,1,0:T(8,128)(2,1)}, u32[]{:S(2)}, u32[]{:S(2)}) collective-permute-start(bf16[2,2,2,128,2048]{4,3,2,1,0:T(8,128)(2,1)} %pad_maximum_fusion.6), channel_id=1, source_target_pairs={{0,1},{1,0},{2,3},{3,2},{4,5},{5,4},{6,7},{7,6},{8,9},{9,8},{10,11... | collective-permute-start | bytes 12582920 | tf_op jit(solution)/shard_map/ppermute | solution.py:420
  400.6 87.2 %collective-permute-start.25 = (bf16[2,512,704]{1,2,0:T(8,128)(2,1)}, bf16[2,512,704]{1,2,0:T(8,128)(2,1)}, u32[]{:S(2)}, u32[]{:S(2)}) collective-permute-start(bf16[2,512,704]{1,2,0:T(8,128)(2,1)} %pad_maximum_fusion.11), channel_id=1, source_target_pairs={{0,8},{8,0},{16,24},{24,16},{1,9},{9,1},{17,25},{25,17},{2,10},{10... | collective-permute-start | bytes 4325384 | tf_op jit(solution)/shard_map/ppermute | solution.py:420
  430.7 126.5 %collective-permute-start.26 = (bf16[2,512,704]{1,2,0:T(8,128)(2,1)}, bf16[2,512,704]{1,2,0:T(8,128)(2,1)}, u32[]{:S(2)}, u32[]{:S(2)}) collective-permute-start(bf16[2,512,704]{1,2,0:T(8,128)(2,1)} %pad_maximum_fusion.11), channel_id=1, source_target_pairs={{0,16},{8,24},{16,0},{24,8},{1,17},{9,25},{17,1},{25,9},{2,18},{10... | collective-permute-start | bytes 4325384 | tf_op jit(solution)/shard_map/ppermute | solution.py:420
  448.9 127.3 %collective-permute-start.22 = (bf16[2,2,2,128,2048]{4,3,2,1,0:T(8,128)(2,1)}, bf16[2,2,2,128,2048]{4,3,2,1,0:T(8,128)(2,1)}, u32[]{:S(2)}, u32[]{:S(2)}) collective-permute-start(bf16[2,2,2,128,2048]{4,3,2,1,0:T(8,128)(2,1)} %pad_maximum_fusion.5), channel_id=1, source_target_pairs={{0,1},{1,0},{2,3},{3,2},{4,5},{5,4},{6,7},{7,6},{8,9},{9,8},{10,11... | collective-permute-start | bytes 12582920 | tf_op jit(solution)/shard_map/ppermute | solution.py:420
  450.6 108.3 %collective-permute-start.27 = (bf16[2,512,704]{1,2,0:T(8,128)(2,1)}, bf16[2,512,704]{1,2,0:T(8,128)(2,1)}, u32[]{:S(2)}, u32[]{:S(2)}) collective-permute-start(bf16[2,512,704]{1,2,0:T(8,128)(2,1)} %pad_maximum_fusion.11), channel_id=1, source_target_pairs={{0,24},{8,16},{16,8},{24,0},{1,25},{9,17},{17,9},{25,1},{2,26},{10... | collective-permute-start | bytes 4325384 | tf_op jit(solution)/shard_map/ppermute | solution.py:420
  630.3 100.0 %collective-permute-start.67 = (bf16[704,512]{1,0:T(8,128)(2,1)}, bf16[704,512]{1,0:T(8,128)(2,1)S(1)}, u32[]{:S(2)}, u32[]{:S(2)}) collective-permute-start(bf16[704,512]{1,0:T(8,128)(2,1)} %fusion.106), channel_id=1, source_target_pairs={{0,24},{8,16},{16,8},{24,0},{1,25},{9,17},{17,9},{25,1},{2,26},{10... | collective-permute-start | bytes 2162696 | tf_op jit(solution)/shard_map/ppermute | solution.py:420
  631.3 99.0 %collective-permute-start.68 = (bf16[704,512]{1,0:T(8,128)(2,1)}, bf16[704,512]{1,0:T(8,128)(2,1)}, u32[]{:S(2)}, u32[]{:S(2)}) collective-permute-start(bf16[704,512]{1,0:T(8,128)(2,1)} %fusion.109), channel_id=1, source_target_pairs={{0,16},{8,24},{16,0},{24,8},{1,17},{9,25},{17,1},{25,9},{2,18},{10... | collective-permute-start | bytes 2162696 | tf_op jit(solution)/shard_map/ppermute | solution.py:420
  657.7 73.6 %collective-permute-start.69 = (bf16[704,512]{1,0:T(8,128)(2,1)}, bf16[704,512]{1,0:T(8,128)(2,1)}, u32[]{:S(2)}, u32[]{:S(2)}) collective-permute-start(bf16[704,512]{1,0:T(8,128)(2,1)} %fusion.112), channel_id=1, source_target_pairs={{0,8},{8,0},{16,24},{24,16},{1,9},{9,1},{17,25},{25,17},{2,10},{10... | collective-permute-start | bytes 2162696 | tf_op jit(solution)/shard_map/ppermute | solution.py:420
  725.3 60.6 %collective-permute-start.63 = (bf16[2,512,704]{1,2,0:T(8,128)(2,1)}, bf16[2,512,704]{1,2,0:T(8,128)(2,1)}, u32[]{:S(2)}, u32[]{:S(2)}) collective-permute-start(bf16[2,512,704]{1,2,0:T(8,128)(2,1)} %pad_maximum_fusion.12), channel_id=1, source_target_pairs={{0,24},{8,16},{16,8},{24,0},{1,25},{9,17},{17,9},{25,1},{2,26},{10... | collective-permute-start | bytes 4325384 | tf_op jit(solution)/shard_map/ppermute | solution.py:420
  728.1 124.8 %collective-permute-start.64 = (bf16[2,512,704]{1,2,0:T(8,128)(2,1)}, bf16[2,512,704]{1,2,0:T(8,128)(2,1)}, u32[]{:S(2)}, u32[]{:S(2)}) collective-permute-start(bf16[2,512,704]{1,2,0:T(8,128)(2,1)} %pad_maximum_fusion.13), channel_id=1, source_target_pairs={{0,16},{8,24},{16,0},{24,8},{1,17},{9,25},{17,1},{25,9},{2,18},{10... | collective-permute-start | bytes 4325384 | tf_op jit(solution)/shard_map/ppermute | solution.py:420
  730.3 131.4 %collective-permute-start.31 = (bf16[2,2,2,128,2048]{4,3,2,1,0:T(8,128)(2,1)}, bf16[2,2,2,128,2048]{4,3,2,1,0:T(8,128)(2,1)S(1)}, u32[]{:S(2)}, u32[]{:S(2)}) collective-permute-start(bf16[2,2,2,128,2048]{4,3,2,1,0:T(8,128)(2,1)} %bitcast.36), channel_id=1, source_target_pairs={{0,1},{1,0},{2,3},{3,2},{4,5},{5,4},{6,7},{7,6},{8,9},{9,8},{10,11... | collective-permute-start | bytes 12582920 | tf_op jit(solution)/shard_map/ppermute | solution.py:420
  771.9 81.0 %collective-permute-start.65 = (bf16[2,512,704]{1,2,0:T(8,128)(2,1)S(1)}, bf16[2,512,704]{1,2,0:T(8,128)(2,1)S(1)}, u32[]{:S(2)}, u32[]{:S(2)}) collective-permute-start(bf16[2,512,704]{1,2,0:T(8,128)(2,1)S(1)} %copy-done.72), channel_id=1, source_target_pairs={{0,8},{8,0},{16,24},{24,16},{1,9},{9,1},{17,25},{25,17},{2,10},{10... | collective-permute-start | bytes 4325384 | tf_op jit(solution)/shard_map/ppermute | solution.py:420
  784.8 70.7 %collective-permute-start.47 = (bf16[2,1,128,2048]{3,2,1,0:T(8,128)(2,1)S(1)}, bf16[2,1,128,2048]{3,2,1,0:T(8,128)(2,1)S(1)}, u32[]{:S(2)}, u32[]{:S(2)}) collective-permute-start(bf16[2,1,128,2048]{3,2,1,0:T(8,128)(2,1)S(1)} %pad_maximum_fusion.26), channel_id=1, source_target_pairs={{0,2},{1,3},{2,0},{3,1},{4,6},{5,7},{6,4},{7,5},{8,10},{9,11},{10,... | collective-permute-start | bytes 3145736 | tf_op jit(solution)/shard_map/ppermute | solution.py:420
  785.9 69.8 %collective-permute-start.49 = (bf16[1,2,128,2048]{3,2,1,0:T(8,128)(2,1)S(1)}, bf16[1,2,128,2048]{3,2,1,0:T(8,128)(2,1)S(1)}, u32[]{:S(2)}, u32[]{:S(2)}) collective-permute-start(bf16[1,2,128,2048]{3,2,1,0:T(8,128)(2,1)S(1)} %pad_maximum_fusion.27), channel_id=1, source_target_pairs={{0,4},{4,0},{1,5},{5,1},{2,6},{6,2},{3,7},{7,3},{8,12},{12,8},{9,1... | collective-permute-start | bytes 3145736 | tf_op jit(solution)/shard_map/ppermute | solution.py:420
  900.0 70.0 %collective-permute-start.33 = (bf16[1,1,128,2048]{3,2,1,0:T(8,128)(2,1)}, bf16[1,1,128,2048]{3,2,1,0:T(8,128)(2,1)}, u32[]{:S(2)}, u32[]{:S(2)}) collective-permute-start(bf16[1,1,128,2048]{3,2,1,0:T(8,128)(2,1)} %slice.1029), channel_id=1, source_target_pairs={{0,4},{4,0},{1,5},{5,1},{2,6},{6,2},{3,7},{7,3},{8,12},{12,8},{9,1... | collective-permute-start | bytes 1572872 | tf_op jit(solution)/shard_map/ppermute | solution.py:420
  955.9 128.3 %collective-permute-start.51 = (bf16[2,2,2,128,2048]{4,3,2,1,0:T(8,128)(2,1)}, bf16[2,2,2,128,2048]{4,3,2,1,0:T(8,128)(2,1)}, u32[]{:S(2)}, u32[]{:S(2)}) collective-permute-start(bf16[2,2,2,128,2048]{4,3,2,1,0:T(8,128)(2,1)} %convolution_convert_fusion), channel_id=1, source_target_pairs={{0,1},{1,0},{2,3},{3,2},{4,5},{5,4},{6,7},{7,6},{8,9},{9,8},{10,11... | collective-permute-start | bytes 12582920 | tf_op jit(solution)/shard_map/ppermute | solution.py:420
  961.1 61.9 %collective-permute-start.60 = (bf16[64,2048]{1,0:T(8,128)(2,1)S(1)}, bf16[64,2048]{1,0:T(8,128)(2,1)S(1)}, u32[]{:S(2)}, u32[]{:S(2)}) collective-permute-start(bf16[64,2048]{1,0:T(8,128)(2,1)S(1)} %get-tuple-element.131), channel_id=1, source_target_pairs={{0,16},{8,24},{16,0},{24,8},{1,17},{9,25},{17,1},{25,9},{2,18},{10... | collective-permute-start | bytes 786440 | tf_op jit(solution)/shard_map/ppermute | solution.py:420
  970.1 57.4 %collective-permute-start.56 = (bf16[512,896]{1,0:T(8,128)(2,1)S(1)}, bf16[512,896]{1,0:T(8,128)(2,1)S(1)}, u32[]{:S(2)}, u32[]{:S(2)}) collective-permute-start(bf16[512,896]{1,0:T(8,128)(2,1)S(1)} %fusion.72), channel_id=1, source_target_pairs={{0,24},{8,16},{16,8},{24,0},{1,25},{9,17},{17,9},{25,1},{2,26},{10... | collective-permute-start | bytes 2752520 | tf_op jit(solution)/shard_map/ppermute | solution.py:420
  972.6 95.4 %collective-permute-start.57 = (bf16[512,896]{1,0:T(8,128)(2,1)S(1)}, bf16[512,896]{1,0:T(8,128)(2,1)S(1)}, u32[]{:S(2)}, u32[]{:S(2)}) collective-permute-start(bf16[512,896]{1,0:T(8,128)(2,1)S(1)} %fusion.75), channel_id=1, source_target_pairs={{0,16},{8,24},{16,0},{24,8},{1,17},{9,25},{17,1},{25,9},{2,18},{10... | collective-permute-start | bytes 2752520 | tf_op jit(solution)/shard_map/ppermute | solution.py:420
  1025.1 75.3 %collective-permute-start.35 = (bf16[1,1,128,2048]{3,2,1,0:T(8,128)(2,1)}, bf16[1,1,128,2048]{3,2,1,0:T(8,128)(2,1)}, u32[]{:S(2)}, u32[]{:S(2)}) collective-permute-start(bf16[1,1,128,2048]{3,2,1,0:T(8,128)(2,1)} %slice.1028), channel_id=1, source_target_pairs={{0,2},{1,3},{2,0},{3,1},{4,6},{5,7},{6,4},{7,5},{8,10},{9,11},{10,... | collective-permute-start | bytes 1572872 | tf_op jit(solution)/shard_map/ppermute | solution.py:420
  1027.5 77.5 %collective-permute-start.62 = (bf16[64,2048]{1,0:T(8,128)(2,1)}, bf16[64,2048]{1,0:T(8,128)(2,1)}, u32[]{:S(2)}, u32[]{:S(2)}) collective-permute-start(bf16[64,2048]{1,0:T(8,128)(2,1)} %fusion.163), channel_id=1, source_target_pairs={{0,0},{8,1},{16,2},{24,3},{1,4},{9,5},{17,6},{25,7},{2,8},{10,9},{... | collective-permute-start | bytes 786440 | tf_op jit(solution)/shard_map/ppermute | solution.py:692
  (183 other events, 3438.0 us)

commit v2 on v1

v2 whole, which is shorter than its diff:
```python
import functools
import jax
import jax.numpy as jnp
from jax import lax
from jax.experimental import pallas as pl
from jax.experimental.pallas import tpu as pltpu
from jax.sharding import Mesh, PartitionSpec as P

KCONV = 4
HD = 128
EPS = 1e-05
UNIT_EPS = 1e-06
F32 = jnp.float32
BF16 = jnp.bfloat16


def mm(left, right, dim_left=1, dim_right=0):
    return lax.dot_general(
        left.astype(BF16),
        right.astype(BF16),
        (((dim_left,), (dim_right,)), ((), ())),
        preferred_element_type=F32,
    )


def split(value):
    high = value.astype(BF16)
    return high, (value - high.astype(F32)).astype(BF16)


def mm3(left, right):
    lh, ll = split(left)
    rh, rl = split(right)
    return mm(lh, rh) + (mm(lh, rl) + mm(ll, rh))


def iota(shape, dim):
    return lax.broadcasted_iota(jnp.int32, shape, dim)


def doc_start(starts, row, place):
    found = jnp.zeros_like(place)
    for j in range(starts.shape[1]):
        first = starts[row, j]
        found = jnp.maximum(found, jnp.where(first <= place, first, 0))
    return found


def scalar_start(starts, row, place):
    found = jnp.int32(0)
    for j in range(starts.shape[1]):
        first = starts[row, j]
        found = jnp.maximum(found, jnp.where(first <= place, first, 0))
    return found


def shift_down(cur, tail, by):
    if by == 0:
        return cur
    rolled = pltpu.roll(cur, by, 0)
    edge = pltpu.roll(tail, by, 0)
    top = jnp.where(iota(edge.shape, 0) < by, edge, rolled[:8])
    return jnp.concatenate([top, rolled[8:]], axis=0)


def shift_up(cur, head, by):
    if by == 0:
        return cur
    size = cur.shape[0]
    rolled = pltpu.roll(cur, size - by, 0)
    edge = pltpu.roll(head, 8 - by, 0)
    last = jnp.where(iota(edge.shape, 0) >= 8 - by, edge, rolled[size - 8 :])
    return jnp.concatenate([rolled[: size - 8], last], axis=0)


class Masks:
    def __init__(self, starts, row, base, size):
        place = base + iota((size, HD), 0)
        start = doc_start(starts, row, place)
        self.inside = [(place - i >= start).astype(F32) for i in range(KCONV)]
        self.carry_in = (start < base).astype(F32)
        last = scalar_start(starts, row, base + size - 1)
        self.last_doc = (start == last).astype(F32)
        self.carry_last = (last < base).astype(F32)
        rows, cols = iota((size, size), 0), iota((size, size), 1)
        start_row = doc_start(starts, row, base + rows)
        start_col = doc_start(starts, row, base + cols)
        same = start_row == start_col
        self.strict = (same & (rows > cols)).astype(F32)
        self.diag = (same & (rows >= cols)).astype(F32)
        self.diag_t = (same & (rows <= cols)).astype(F32)


def conv_of(cur, tail, taps, masks):
    shifted = [shift_down(cur, tail, i) * masks.inside[i] for i in range(KCONV)]
    total = shifted[0] * taps[0:1]
    for i in range(1, KCONV):
        total = total + shifted[i] * taps[i : i + 1]
    return shifted, total


def unit(values):
    return lax.rsqrt(jnp.sum(values * values, axis=-1, keepdims=True) + UNIT_EPS)


def inverse(lowers, size):
    rows, cols = iota((size, size), 0), iota((size, size), 1)
    eye = (rows == cols).astype(F32)
    near = (rows // 16) == (cols // 16)
    lows = [jnp.where(near, lower, 0.0) for lower in lowers]
    founds = [eye - low for low in lows]
    squares = [mm3(low, low) for low in lows]
    for level in range(3):
        if level:
            squares = [mm3(square, square) for square in squares]
        founds = [found + mm3(found, square) for found, square in zip(founds, squares)]
    width = 16
    while width < size:
        near = ((rows // (2 * width)) == (cols // (2 * width))) & ((rows // width) != (cols // width))
        crosses = [mm3(found, jnp.where(near, lower, 0.0)) for found, lower in zip(founds, lowers)]
        founds = [found - mm3(cross, found) for found, cross in zip(founds, crosses)]
        width *= 2
    return founds


def forward_kernel(heads, rows, size, starts, place, lin, taps, gain, low_out, mixed_out, inv_out, fix_out, err_out, mem_out, memory, tails):
    step = pl.program_id(0)
    base = step * size

    @pl.when(step == 0)
    def _():
        memory[...] = jnp.zeros_like(memory)
        tails[...] = jnp.zeros_like(tails)

    every_mask = [Masks(starts, row, base, size) for row in range(rows)]
    pairs = [(row, head) for row in range(rows) for head in range(heads)]

    def group(row, head, kind):
        at = (kind * heads + head) * HD
        cur = lin[0, 0, row, 0, :, at : at + HD].astype(BF16).astype(F32)
        tail = tails[row, :, at : at + HD]
        _, conv = conv_of(cur, tail, taps[:, at : at + HD], every_mask[row])
        tails[row, :, at : at + HD] = cur[size - 8 :]
        return conv * jax.nn.sigmoid(conv)

    def rate_of(row, head):
        at = 3 * heads * HD + head
        return jnp.broadcast_to(jax.nn.sigmoid(lin[0, 0, row, 0, :, at : at + 1]), (size, HD))

    queries = [group(row, head, 0) for row, head in pairs]
    keys = [group(row, head, 1) for row, head in pairs]
    queries = [query * unit(query) for query in queries]
    keys = [key * unit(key) for key in keys]
    rates = [rate_of(row, head) for row, head in pairs]
    grams = [mm(jnp.concatenate([query, key], axis=0), key, 1, 1) for query, key in zip(queries, keys)]
    lowers = [
        (rate if size == HD else rate[:, :size]) * gram[size:] * every_mask[row].strict
        for (row, _), rate, gram in zip(pairs, rates, grams)
    ]
    inverses = inverse(lowers, size)
    for pair, (row, head) in enumerate(pairs):
        inv_out[0, pair] = inverses[pair].astype(BF16)
        mem_out[0, pair] = memory[pair]
    values = [group(row, head, 2) for row, head in pairs]
    reads = [
        mm(jnp.concatenate([query, key], axis=0), memory[pair])
        for pair, (query, key) in enumerate(zip(queries, keys))
    ]
    errors = [
        value - every_mask[row].carry_in * read[size:] for (row, _), value, read in zip(pairs, values, reads)
    ]
    fixes = [mm(inv, rate * error) for inv, rate, error in zip(inverses, rates, errors)]
    mixes = [
        every_mask[row].carry_in * read[:size] + mm(gram[:size] * every_mask[row].diag, fix)
        for (row, _), read, gram, fix in zip(pairs, reads, grams, fixes)
    ]
    for pair, (row, head) in enumerate(pairs):
        masks = every_mask[row]
        memory[pair] = masks.carry_last * memory[pair] + mm(keys[pair] * masks.last_doc, fixes[pair], 0, 0)
        fix_out[0, pair] = fixes[pair]
        err_out[0, pair] = errors[pair]
        mixed = mixes[pair]
        stat = lax.rsqrt(jnp.mean(mixed * mixed, axis=-1, keepdims=True) + EPS)
        at = head * HD
        low_out[0, 0, row, 0, :, at : at + HD] = (mixed * stat * gain[:, at : at + HD]).astype(BF16)
        mixed_out[0, 0, row, 0, :, at : at + HD] = mixed


def backward_kernel(heads, rows, size, steps, starts, place, lin, edge, taps, gain, mixed_in, grad_in, inv_in, fix_in, err_in, mem_in, dlin_out, dtaps_out, dgain_out, dmemory, nexts):
    step = pl.program_id(0)
    chunk = steps - 1 - step
    base = chunk * size

    @pl.when(step == 0)
    def _():
        dmemory[...] = jnp.zeros_like(dmemory)
        nexts[...] = jnp.zeros_like(nexts)
        dtaps_out[...] = jnp.zeros_like(dtaps_out)
        dgain_out[...] = jnp.zeros_like(dgain_out)

    pairs = [(row, head) for row in range(rows) for head in range(heads)]
    each = range(len(pairs))
    every_mask = [Masks(starts, row, base, size) for row in range(rows)]
    masks = [every_mask[row] for row, _ in pairs]
    next_place = base + size + iota((8, HD), 0)
    next_starts = [doc_start(starts, row, next_place) for row in range(rows)]
    inside_next = [[(next_place - i >= start).astype(F32) for i in range(KCONV)] for start in next_starts]

    def group(row, head, kind):
        at = (kind * heads + head) * HD
        cur = lin[0, 0, row, 0, :, at : at + HD].astype(BF16).astype(F32)
        tail = edge[0, 0, row, 0, :, at : at + HD].astype(BF16).astype(F32)
        shifted, conv = conv_of(cur, tail, taps[:, at : at + HD], every_mask[row])
        sig = jax.nn.sigmoid(conv)
        return shifted, conv * sig, sig * (1.0 + conv * (1.0 - sig))

    def group_back(row, head, kind, grad):
        at = (kind * heads + head) * HD
        shifted, _, slope = group(row, head, kind)
        dconv = grad * slope
        after = nexts[row, :, at : at + HD]
        total = None
        for i in range(KCONV):
            dtaps_out[i : i + 1, at : at + HD] += jnp.sum(shifted[i] * dconv, axis=0, keepdims=True)
            back = (
                shift_up(dconv * every_mask[row].inside[i], after * inside_next[row][i], i)
                * taps[i : i + 1, at : at + HD]
            )
            total = back if total is None else total + back
        nexts[row, :, at : at + HD] = dconv[:8]
        dlin_out[0, 0, row, 0, :, at : at + HD] = total.astype(BF16)

    def head_back(row, head):
        at = head * HD
        mixed = mixed_in[0, 0, row, 0, :, at : at + HD]
        dhead = grad_in[0, 0, row, 0, :, at : at + HD].astype(F32)
        stat = lax.rsqrt(jnp.mean(mixed * mixed, axis=-1, keepdims=True) + EPS)
        scaled = mixed * stat
        dgain_out[:, at : at + HD] += jnp.sum(dhead * scaled, axis=0, keepdims=True)
        weighted = dhead * gain[:, at : at + HD]
        return stat * (weighted - scaled * jnp.mean(weighted * scaled, axis=-1, keepdims=True))

    def rate_of(row, head):
        at = 3 * heads * HD + head
        return jnp.broadcast_to(jax.nn.sigmoid(lin[0, 0, row, 0, :, at : at + 1]), (size, HD))

    queries = [group(row, head, 0)[1] for row, head in pairs]
    keys = [group(row, head, 1)[1] for row, head in pairs]
    q_units, k_units = [unit(query) for query in queries], [unit(key) for key in keys]
    queries = [query * u for query, u in zip(queries, q_units)]
    keys = [key * u for key, u in zip(keys, k_units)]
    rates = [rate_of(row, head) for row, head in pairs]
    dmixes = [head_back(row, head) for row, head in pairs]
    grams = [mm(key, jnp.concatenate([key, query], axis=0), 1, 1) for query, key in zip(queries, keys)]
    dfixes = [
        mm(grams[p][:, size:] * masks[p].diag_t, dmixes[p]) + mm(keys[p] * masks[p].last_doc, dmemory[p])
        for p in each
    ]
    drights = [mm(inv_in[0, p], dfixes[p], 0, 0) for p in each]
    boths = [mm(jnp.concatenate([dmixes[p], -drights[p]], axis=0), fix_in[0, p], 1, 1) for p in each]
    dattends = [boths[p][:size] * masks[p].diag for p in each]
    dlowers = [boths[p][size:] * masks[p].strict for p in each]
    drates = [
        jnp.sum(drights[p] * err_in[0, p], axis=-1, keepdims=True)
        + jnp.sum(dlowers[p] * grams[p][:, :size], axis=-1, keepdims=True)
        for p in each
    ]
    dreads = [
        jnp.concatenate([masks[p].carry_in * dmixes[p], -(rates[p] * masks[p].carry_in * drights[p])], axis=0)
        for p in each
    ]
    from_states = [mm(dreads[p], mem_in[0, p], 1, 1) for p in each]
    dlowers = [dlowers[p] * (rates[p] if size == HD else rates[p][:, :size]) for p in each]
    dqueries = [from_states[p][:size] + mm(dattends[p], keys[p]) for p in each]
    dkeys = [
        from_states[p][size:]
        + mm(dattends[p], queries[p], 0, 0)
        + mm(dlowers[p] + dlowers[p].T, keys[p])
        + masks[p].last_doc * mm(fix_in[0, p], dmemory[p], 1, 1)
        for p in each
    ]
    for p in each:
        dmemory[p] = masks[p].carry_last * dmemory[p] + mm(
            jnp.concatenate([queries[p], keys[p]], axis=0), dreads[p], 0, 0
        )
    lanes = iota((size, HD), 1)
    rate_grads = [jnp.zeros((size, HD), F32)] * rows
    for p, (row, head) in enumerate(pairs):
        dquery = q_units[p] * (dqueries[p] - queries[p] * jnp.sum(dqueries[p] * queries[p], axis=-1, keepdims=True))
        dkey = k_units[p] * (dkeys[p] - keys[p] * jnp.sum(dkeys[p] * keys[p], axis=-1, keepdims=True))
        group_back(row, head, 0, dquery)
        group_back(row, head, 1, dkey)
        group_back(row, head, 2, rates[p] * drights[p])
        rate_grads[row] = jnp.where(lanes == head, drates[p] * rates[p] * (1.0 - rates[p]), rate_grads[row])
    at = 3 * heads * HD
    for row in range(rows):
        dlin_out[0, 0, row, 0, :, at : at + HD] = rate_grads[row].astype(BF16)


def chunk_at(step, place):
    block = (step // 2) ^ place[0]
    return block % 2, step % 2, block // 2


def delta_forward(lin, taps, gain, starts, place, heads, layout):
    cores, halves, rows, folds, size = layout
    steps = cores * halves * folds
    pairs = rows * heads
    wide = lin.shape[1]

    def at_chunk(step, starts, place):
        core, half, fold = chunk_at(step, place)
        return core, half, 0, fold, 0, 0

    def token_block(columns):
        return pl.BlockSpec((1, 1, rows, 1, size, columns), at_chunk)

    def saved(columns, tall):
        return pl.BlockSpec((1, pairs, tall, columns), lambda step, starts, place: (step, 0, 0, 0))

    def tokens(columns, kind):
        return jax.ShapeDtypeStruct(layout + (columns,), kind)

    total = cores * halves * rows * folds * size
    outs = pl.pallas_call(
        functools.partial(forward_kernel, heads, rows, size),
        grid_spec=pltpu.PrefetchScalarGridSpec(
            num_scalar_prefetch=2,
            grid=(steps,),
            in_specs=[
                token_block(wide),
                pl.BlockSpec(taps.shape, lambda step, starts, place: (0, 0)),
                pl.BlockSpec(gain.shape, lambda step, starts, place: (0, 0)),
            ],
            out_specs=[
                token_block(heads * HD),
                token_block(heads * HD),
                saved(size, size),
                saved(HD, size),
                saved(HD, size),
                saved(HD, HD),
            ],
            scratch_shapes=[
                pltpu.VMEM((pairs, HD, HD), F32),
                pltpu.VMEM((rows, 8, 3 * heads * HD), F32),
            ],
        ),
        out_shape=[
            tokens(heads * HD, BF16),
            tokens(heads * HD, F32),
            jax.ShapeDtypeStruct((steps, pairs, size, size), BF16),
            jax.ShapeDtypeStruct((steps, pairs, size, HD), F32),
            jax.ShapeDtypeStruct((steps, pairs, size, HD), F32),
            jax.ShapeDtypeStruct((steps, pairs, HD, HD), F32),
        ],
        compiler_params=pltpu.CompilerParams(
            dimension_semantics=("arbitrary",), vmem_limit_bytes=40 * 1024 * 1024
        ),
        cost_estimate=pl.CostEstimate(
            flops=total * HD * HD * heads * 600, bytes_accessed=total * wide * 8, transcendentals=0
        ),
        name="delta_forward",
    )(starts, place, lin.reshape(layout + (wide,)), taps, gain)
    low, mixed = outs[:2]
    return low.reshape(total, heads * HD), mixed, tuple(outs[2:])


def delta_backward(lin, taps, gain, starts, place, mixed, dhead, saves, heads, layout):
    cores, halves, rows, folds, size = layout
    steps = cores * halves * folds
    pairs = rows * heads
    wide = lin.shape[1]
    total = cores * halves * rows * folds * size

    def at_chunk(step, starts, place):
        core, half, fold = chunk_at(steps - 1 - step, place)
        return core, half, 0, fold, 0, 0

    def at_edge(step, starts, place):
        core, half, fold = chunk_at(jnp.maximum(steps - 2 - step, 0), place)
        return core, half, 0, fold, size // 8 - 1, 0

    def token_block(columns):
        return pl.BlockSpec((1, 1, rows, 1, size, columns), at_chunk)

    def saved(columns, tall):
        return pl.BlockSpec((1, pairs, tall, columns), lambda step, starts, place: (steps - 1 - step, 0, 0, 0))

    whole = lambda step, starts, place: (0, 0)
    lin_blocks = lin.reshape(layout + (wide,))
    dlin, dtaps, dgain = pl.pallas_call(
        functools.partial(backward_kernel, heads, rows, size, steps),
        grid_spec=pltpu.PrefetchScalarGridSpec(
            num_scalar_prefetch=2,
            grid=(steps,),
            in_specs=[
                token_block(wide),
                pl.BlockSpec((1, 1, rows, 1, 8, wide), at_edge),
                pl.BlockSpec(taps.shape, whole),
                pl.BlockSpec(gain.shape, whole),
                token_block(heads * HD),
                token_block(heads * HD),
                saved(size, size),
                saved(HD, size),
                saved(HD, size),
                saved(HD, HD),
            ],
            out_specs=[
                token_block(wide),
                pl.BlockSpec(taps.shape, whole),
                pl.BlockSpec(gain.shape, whole),
            ],
            scratch_shapes=[
                pltpu.VMEM((pairs, HD, HD), F32),
                pltpu.VMEM((rows, 8, 3 * heads * HD), F32),
            ],
        ),
        out_shape=[
            jax.ShapeDtypeStruct(layout + (wide,), BF16),
            jax.ShapeDtypeStruct(taps.shape, F32),
            jax.ShapeDtypeStruct(gain.shape, F32),
        ],
        compiler_params=pltpu.CompilerParams(
            dimension_semantics=("arbitrary",), vmem_limit_bytes=40 * 1024 * 1024
        ),
        cost_estimate=pl.CostEstimate(
            flops=total * HD * HD * heads * 700, bytes_accessed=total * wide * 10, transcendentals=0
        ),
        name="delta_backward",
    )(starts, place, lin_blocks, lin_blocks, taps, gain, mixed, dhead.reshape(layout + (heads * HD,)), *saves)
    return dlin.reshape(total, wide), dtaps, dgain


def partner(value, axis, bit):
    count = lax.axis_size(axis)
    return lax.ppermute(value, axis, [(i, i ^ bit) for i in range(count)])


OUTER = [(1, 0), (2, 3)]
INNER = [(0, 1), (3, 2)]
MIDDLE = [(1, 2), (2, 1)]


class Flight:
    def __init__(self, steps):
        self.steps = steps
        self.parts = next(steps)
        self.result = None

    def advance(self):
        try:
            self.parts = self.steps.send(self.parts)
        except StopIteration as end:
            self.parts, self.result = None, end.value

    def join(self, value):
        if self.parts is None:
            return value
        value, self.parts = lax.optimization_barrier((value, self.parts))
        self.advance()
        return value

    def land(self, *others):
        for other in others:
            self.parts = other.join(self.parts)
        self.advance()
        return self.result


def joined(value, *flights):
    for flight in flights:
        value = flight.join(value)
    return value


def gather_z(piece):
    count = lax.axis_size("z")
    if count == 4:
        one, three = yield [partner(piece, "z", 1), lax.ppermute(piece, "z", MIDDLE)]
        two, far = yield [lax.ppermute(three, "z", OUTER), lax.ppermute(one, "z", MIDDLE)]
        (last,) = yield [lax.ppermute(far, "z", OUTER)]
        return [piece, one, two + far, three + last]
    pieces = yield [partner(piece, "z", k) for k in range(1, count)]
    return [piece] + pieces


def sum_z(blocks):
    count = lax.axis_size("z")
    if count == 4:
        own, one, two, three = blocks
        (far,) = yield [lax.ppermute(three.astype(BF16), "z", INNER)]
        near, far = yield [
            lax.ppermute(two.astype(BF16), "z", INNER),
            lax.ppermute((two.astype(F32) + far.astype(F32)).astype(BF16), "z", MIDDLE),
        ]
        one, three = yield [
            partner((one.astype(F32) + far.astype(F32)).astype(BF16), "z", 1),
            lax.ppermute((three.astype(F32) + near.astype(F32)).astype(BF16), "z", MIDDLE),
        ]
        return own.astype(F32) + one.astype(F32) + three.astype(F32)
    parts = yield [partner(blocks[k].astype(BF16), "z", k) for k in range(1, count)]
    total = blocks[0].astype(F32)
    for part in parts:
        total = total + part.astype(F32)
    return total


def swapped_z(blocks, place):
    bit = 1
    while bit < len(blocks):
        odd = (place & bit) != 0
        blocks = [jnp.where(odd, blocks[k ^ bit], blocks[k]) for k in range(len(blocks))]
        bit *= 2
    return blocks


def permute_z(array):
    count = lax.axis_size("z")
    size = array.shape[1] // count
    blocks = [array[:, k * size : (k + 1) * size] for k in range(count)]
    return jnp.concatenate(swapped_z(blocks, lax.axis_index("z")), axis=1)


def steps_of(half):
    folds = lax.axis_size("s") // 2
    along_y = []
    bit = 2
    while bit < 2 * folds:
        along_y.append(("s", bit))
        bit *= 2
    return [("x", 1)] + along_y if half == 0 else along_y + [("x", 1)]


def axis_of(step):
    axis, bit = step
    return 0 if axis == "x" else 1


def gather_group(own):
    tokens, wide = own.shape
    parts = [own[: tokens // 2].reshape(1, 1, tokens // 2, wide), own[tokens // 2 :].reshape(1, 1, tokens // 2, wide)]
    plans = [steps_of(0), steps_of(1)]
    for number in range(len(plans[0])):
        arrived = yield [partner(part, *plan[number]) for part, plan in zip(parts, plans)]
        parts = [
            jnp.concatenate([part, other], axis=axis_of(plan[number]))
            for part, other, plan in zip(parts, arrived, plans)
        ]
    mine = jnp.stack(parts)
    (theirs,) = yield [partner(mine, "s", 1)]
    return jnp.concatenate([mine, theirs], axis=0).reshape(-1, wide)


def scatter_group(mine, theirs):
    _, _, folds, size, wide = mine.shape
    (arrived,) = yield [partner(theirs.astype(BF16), "s", 1)]
    total = mine.astype(F32) + arrived.astype(F32)
    parts = [total[0], total[1]]
    plans = [steps_of(0)[::-1], steps_of(1)[::-1]]
    for number in range(len(plans[0])):
        sends, keeps = [], []
        for part, plan in zip(parts, plans):
            dim = axis_of(plan[number])
            count = part.shape[dim] // 2
            keeps.append(lax.slice_in_dim(part, 0, count, axis=dim))
            sends.append(lax.slice_in_dim(part, count, 2 * count, axis=dim))
        arrived = yield [partner(send.astype(BF16), *plan[number]) for send, plan in zip(sends, plans)]
        parts = [keep + other.astype(F32) for keep, other in zip(keeps, arrived)]
    return jnp.concatenate([part.reshape(size, wide) for part in parts], axis=0)


def ended(flight):
    while flight.parts is not None:
        flight.advance()
    return flight.result


def norm_back(grad_out, scaled, stat, gain):
    weighted = grad_out * gain
    gain_grad = jnp.sum(grad_out * scaled, axis=0)
    input_grad = stat * (weighted - scaled * jnp.mean(weighted * scaled, axis=-1, keepdims=True))
    return (input_grad, gain_grad)


def dot(left, right, dim_left=1, dim_right=0):
    return lax.dot_general(left, right, (((dim_left,), (dim_right,)), ((), ())), preferred_element_type=F32)


def after(value, *others):
    return lax.optimization_barrier((value,) + others)[0]


def body(
    hidden_in,
    doc_lengths,
    norm1_gain,
    w_qkv,
    conv_weight,
    w_beta,
    head_gain,
    w_out,
    norm2_gain,
    w_gate_up,
    w_down,
    cotangent,
):
    deep, pair, seq = lax.axis_size("z"), lax.axis_size("x"), lax.axis_size("s")
    place_z, place_x, place_s = lax.axis_index("z"), lax.axis_index("x"), lax.axis_index("s")
    team = pair * seq
    devices = deep * team
    place = place_x * seq + place_s
    tokens, wide = hidden_in.shape[1:]
    folds, size = seq // 2, tokens // 2
    layout = (2, 2, pair, folds, size)
    rows_each = w_qkv.shape[0]
    total_heads = w_beta.shape[1]
    heads = total_heads // team
    span = heads * HD
    block = wide // deep
    taps_each = conv_weight.shape[1]

    cut = w_qkv.reshape(rows_each, 3, team, span).transpose(2, 0, 1, 3).reshape(team, rows_each, 3 * span)
    cut = lax.all_to_all(cut, ("x", "s"), 0, 0, tiled=True).reshape(team * rows_each, 3 * span)

    small = jnp.concatenate(
        [
            norm1_gain,
            norm2_gain,
            head_gain,
            conv_weight.reshape(-1),
            w_beta.reshape(-1),
        ]
    )
    length = small.shape[0]
    padded = -(-length // 128) * 128
    small = jnp.pad(small, (0, padded - length))
    small = lax.all_to_all(
        jnp.broadcast_to(after(small, cut)[None], (devices, padded)), ("z", "x", "s"), 0, 0, tiled=True
    )
    out_from = [(i, (i % deep) * team + i // deep) for i in range(devices)]

    def gather_out(piece):
        (piece,) = yield [lax.ppermute(piece, ("z", "x", "s"), out_from)]
        return (yield from gather_z(piece))

    units = w_gate_up.shape[2] // pair
    second = place_x == 1

    def swap_x(array, axis):
        low_part = lax.slice_in_dim(array, 0, units, axis=axis)
        high_part = lax.slice_in_dim(array, units, 2 * units, axis=axis)
        mine = jnp.where(second, high_part, low_part)
        (theirs,) = yield [partner(jnp.where(second, low_part, high_part), "x", 1)]
        return jnp.concatenate([jnp.where(second, theirs, mine), jnp.where(second, mine, theirs)], axis=1)

    starts = jnp.sum(
        jnp.where(
            jnp.arange(doc_lengths.shape[1])[None, :] < jnp.arange(doc_lengths.shape[1])[:, None],
            doc_lengths[0][None, :],
            0,
        ),
        axis=1,
    )[None]
    starts = jnp.concatenate([starts, partner(starts, "x", 1)], axis=0)
    place_seq = place_s.reshape(1).astype(jnp.int32)

    hidden_flight = Flight(gather_group(permute_z(hidden_in[0])))
    hidden_flight.parts, cut = lax.optimization_barrier((hidden_flight.parts, cut))
    hidden_flight.advance()
    qkv_flight = Flight(gather_z(cut))
    gu_swap = Flight(swap_x(w_gate_up.transpose(1, 0, 2), 2))
    hidden_flight.parts, small = lax.optimization_barrier((hidden_flight.parts, small))
    hidden_flight.land(qkv_flight, gu_swap)
    gain_one = small[:, :rows_each].reshape(1, wide).astype(F32)
    gain_two = small[:, rows_each : 2 * rows_each].reshape(1, wide).astype(F32)
    gain_head = lax.dynamic_slice_in_dim(
        small[:, 2 * rows_each : 3 * rows_each].reshape(1, wide), place * span, span, axis=1
    ).astype(F32)
    at = 3 * rows_each
    taps = small[:, at : at + KCONV * taps_each].reshape(devices, KCONV, taps_each)
    taps = taps.transpose(1, 0, 2).reshape(KCONV, 3, team, span)
    taps = lax.dynamic_index_in_dim(taps, place, 2, False).reshape(KCONV, 3 * span).astype(F32)
    at = at + KCONV * taps_each
    betas = small[:, at:length].reshape(deep, team * rows_each, total_heads)
    betas = swapped_z(list(lax.dynamic_slice_in_dim(betas, place * heads, heads, axis=2)), place_z)
    betas = jnp.pad(jnp.concatenate(betas, axis=0), ((0, 0), (0, HD - heads)))

    down_swap = Flight(swap_x(w_down, 0))
    out_flight = Flight(gather_out(after(w_out, cut)))
    hidden_flight.land(qkv_flight, down_swap, out_flight)
    hidden_all = ended(hidden_flight).astype(F32)
    gain_one_z = permute_z(gain_one)
    stat_all = lax.rsqrt(jnp.mean(hidden_all * hidden_all, axis=-1, keepdims=True) + EPS)
    normed_one = joined((hidden_all * stat_all * gain_one_z).astype(BF16), qkv_flight, out_flight)
    mat_qkv = jnp.concatenate([jnp.concatenate(ended(qkv_flight), axis=0), betas], axis=1)
    normed_one, gu_piece, down_piece, cot_rows = lax.optimization_barrier(
        (normed_one, gu_swap.result, down_swap.result, cotangent[0])
    )
    gu_flight = Flight(gather_z(gu_piece))
    cot_flight = Flight(gather_group(permute_z(cot_rows)))
    linear = joined(dot(normed_one, mat_qkv), out_flight, cot_flight)
    head_low, mixed, saves = delta_forward(linear, taps, gain_head, starts, place_seq, heads, layout)
    head_low = joined(head_low, gu_flight, out_flight, cot_flight)
    mat_out = jnp.concatenate(swapped_z(ended(out_flight), place_z), axis=0)
    half_rows = head_low.shape[0] // 2
    part_shape = (2, pair, folds, size, wide)
    attn_flight = Flight(
        scatter_group(
            dot(head_low[:half_rows], mat_out).reshape(part_shape),
            dot(head_low[half_rows:], mat_out).reshape(part_shape),
        )
    )
    attn_flight.land(cot_flight)
    attn_flight.land(gu_flight)
    down_flight = Flight(gather_z(after(down_piece, attn_flight.parts)))
    while attn_flight.parts is not None:
        attn_flight.land()
    resid = hidden_in[0].astype(F32)
    middle = resid + attn_flight.result
    stat_two = lax.rsqrt(jnp.mean(middle * middle, axis=-1, keepdims=True) + EPS)
    scaled_two = middle * stat_two

    cot_all = ended(cot_flight)
    normed_flight = Flight(gather_group(permute_z((scaled_two * gain_two).astype(BF16))))
    normed_flight.land(gu_flight)
    while normed_flight.parts is not None:
        normed_flight.land(down_flight)
    normed_two = normed_flight.result
    mat_gu = jnp.concatenate(ended(gu_flight), axis=1)
    mat_gate, mat_up = mat_gu[0], mat_gu[1]
    gate = dot(normed_two, mat_gate)
    upper = down_flight.join(dot(normed_two, mat_up))
    mat_down = jnp.concatenate(ended(down_flight), axis=1)

    def columns(array, k):
        return array[:, k * block : (k + 1) * block]

    sig_gate = jax.nn.sigmoid(gate)
    act_low = (gate * sig_gate * upper).astype(BF16)
    act_grad = dot(cot_all, mat_down, 1, 1)
    gate_grad = (act_grad * upper * sig_gate * (1.0 + gate * (1.0 - sig_gate))).astype(BF16)
    upper_grad = (act_grad * gate * sig_gate).astype(BF16)

    def into_group(rows):
        return (dot(gate_grad[rows], mat_gate, 1, 1) + dot(upper_grad[rows], mat_up, 1, 1)).reshape(part_shape)

    grads_theirs = into_group(slice(half_rows, None)).astype(BF16)
    grads_mine = into_group(slice(0, half_rows))
    grad_flight = Flight(scatter_group(grads_mine, grads_theirs))
    act_low, cot_all, normed_two, grads_theirs = lax.optimization_barrier((act_low, cot_all, normed_two, grads_theirs))

    def down_block(k):
        return dot(act_low, columns(cot_all, k), 0, 0).astype(BF16)

    def gu_block(k):
        rows = columns(normed_two, k)
        return jnp.stack([dot(rows, gate_grad, 0, 0).astype(BF16), dot(rows, upper_grad, 0, 0).astype(BF16)])

    down_sum = Flight(sum_z([down_block(k) for k in range(deep)]))
    gu_sum = Flight(sum_z([gu_block(k) for k in range(deep)]))
    grad_flight.land()
    grad_flight.land(down_sum)
    grad_flight.land(gu_sum)
    normed_two_grad = permute_z(ended(grad_flight))
    ffn_flight = Flight(
        scatter_group(
            dot(act_low[:half_rows], mat_down).reshape(part_shape),
            dot(act_low[half_rows:], mat_down).reshape(part_shape),
        )
    )

    def back_x(array, axis, join):
        half = array.shape[axis] // 2
        low_part = lax.slice_in_dim(array, 0, half, axis=axis)
        high_part = lax.slice_in_dim(array, half, 2 * half, axis=axis)
        mine = jnp.where(second, high_part, low_part)
        (theirs,) = yield [partner(jnp.where(second, low_part, high_part).astype(BF16), "x", 1)]
        theirs = theirs.astype(F32)
        return jnp.concatenate(
            [jnp.where(second, theirs, mine), jnp.where(second, mine, theirs)], axis=join
        )

    middle_part, gain_two_grad = norm_back(normed_two_grad, scaled_two, stat_two, gain_two)
    middle_grad = cot_rows.astype(F32) + middle_part

    dattn_flight = Flight(gather_group(middle_grad.astype(BF16)))
    dattn_flight.land(down_sum)
    dattn_flight.land(gu_sum, ffn_flight)
    attn_low = ended(dattn_flight)
    head_grad = joined(dot(attn_low, mat_out, 1, 1), down_sum)
    out_part = dot(head_low, attn_low, 0, 0).astype(BF16).reshape(deep, span // deep, wide)
    out_sum = Flight(sum_z(swapped_z(list(out_part), place_z)))
    down_back = Flight(back_x(ended(down_sum), 1, 0))
    lin_grad, taps_grad, gain_head_grad = delta_backward(
        linear, taps, gain_head, starts, place_seq, mixed, head_grad, saves, heads, layout
    )
    lin_grad = joined(lin_grad, gu_sum, out_sum, ffn_flight, down_back)
    gu_back = Flight(back_x(ended(gu_sum), 1, 2))

    def qkv_block(k):
        return dot(columns(normed_one, k), lin_grad[:, : 3 * span], 0, 0).astype(BF16)

    qkv_blocks = [qkv_block(k) for k in range(deep)]
    qkv_sum = Flight(sum_z(qkv_blocks))
    lin_grad_next, _ = lax.optimization_barrier((lin_grad, qkv_blocks[-1]))
    grads_theirs = dot(lin_grad_next[half_rows:], mat_qkv, 1, 1).astype(BF16).reshape(part_shape)
    grads_mine = dot(lin_grad_next[:half_rows], mat_qkv, 1, 1).reshape(part_shape)
    grads_mine = joined(grads_mine, qkv_sum, out_sum)
    last_flight = Flight(scatter_group(grads_mine, grads_theirs))
    last_flight.land(gu_back)
    last_flight.land(qkv_sum, out_sum, ffn_flight)
    beta_part = dot(normed_one, lin_grad[:, 3 * span :], 0, 0)[:, :heads]
    normed_grad = permute_z(ended(last_flight))
    stat_one = lax.rsqrt(jnp.mean(resid * resid, axis=-1, keepdims=True) + EPS)
    resid_part, _ = norm_back(normed_grad, resid * stat_one, stat_one, gain_one)
    input_grad = middle_grad + resid_part
    result = (middle + permute_z(ended(ffn_flight))).astype(BF16)
    gu_weight_grad = ended(gu_back).transpose(1, 0, 2)
    down_weight_grad = ended(down_back)
    out_weight_grad = lax.ppermute(
        ended(out_sum).astype(BF16), ("z", "x", "s"), [(b, a) for a, b in out_from]
    ).astype(F32)
    qkv_back = lax.all_to_all(
        ended(qkv_sum).astype(BF16).reshape(team, rows_each, 3 * span), ("x", "s"), 0, 0, tiled=True
    ).astype(F32)
    qkv_weight_grad = (
        qkv_back.reshape(team, rows_each, 3, span).transpose(1, 2, 0, 3).reshape(rows_each, 3 * wide)
    )

    head_full = lax.dynamic_update_slice(jnp.zeros((1, wide), F32), gain_head_grad, (0, place * span))
    taps_full = lax.dynamic_update_slice(
        jnp.zeros((KCONV, 3, team, span), F32),
        taps_grad.reshape(KCONV, 3, 1, span),
        (0, 0, place, 0),
    )
    taps_full = taps_full.reshape(KCONV, devices, taps_each).transpose(1, 0, 2).reshape(devices, KCONV * taps_each)
    beta_part = jnp.concatenate(swapped_z(list(beta_part.reshape(deep, block, heads)), place_z), axis=0)
    beta_full = lax.dynamic_update_slice(jnp.zeros((wide, total_heads), F32), beta_part, (0, place * heads))
    small_grads = jnp.concatenate(
        [
            gain_two_grad.reshape(devices, rows_each),
            head_full.reshape(devices, rows_each),
            taps_full,
            beta_full.reshape(devices, rows_each * total_heads),
        ],
        axis=1,
    )
    length = small_grads.shape[1]
    small_grads = jnp.pad(small_grads, ((0, 0), (0, -length % 128)))
    small_grads = jnp.sum(
        lax.all_to_all(small_grads, ("z", "x", "s"), 0, 0, tiled=True), axis=0
    )
    at = 2 * rows_each + KCONV * taps_each
    beta_weight_grad = small_grads[at:length].reshape(rows_each, total_heads)
    gain_one_grad = (
        jnp.sum(w_qkv.astype(F32) * qkv_weight_grad, axis=1)
        + jnp.sum(w_beta.astype(F32) * beta_weight_grad, axis=1)
    ) / norm1_gain.astype(F32)
    return (
        result[None],
        input_grad[None],
        gain_one_grad,
        qkv_weight_grad,
        small_grads[2 * rows_each : at].reshape(KCONV, taps_each),
        beta_weight_grad,
        small_grads[rows_each : 2 * rows_each],
        out_weight_grad,
        small_grads[:rows_each],
        gu_weight_grad,
        down_weight_grad,
    )


def solution(mesh):
    outer, seq = mesh.shape["dp"], mesh.shape["seq"]
    grid = Mesh(mesh.devices.reshape(outer // 2, 2, seq), ("z", "x", "s"))
    every = ("z", "x", "s")
    rows = ("z", "x")
    in_specs = (
        P(rows, "s", None),
        P(rows, None),
        P(every),
        P(every, None),
        P(None, every),
        P(every, None),
        P(every),
        P(every, None),
        P(every),
        P(rows, None, "s"),
        P("s", rows),
        P(rows, "s", None),
    )
    out_specs = (
        P(rows, "s", None),
        P(rows, "s", None),
        P(every),
        P(every, None),
        P(None, every),
        P(every, None),
        P(every),
        P(every, None),
        P(every),
        P(rows, None, "s"),
        P("s", rows),
    )
    return jax.shard_map(body, mesh=grid, in_specs=in_specs, out_specs=out_specs, check_vma=False)
```

time: 1170 us -> 851 us (0.73)
  waiting for transfers between devices: 562 us -> 208 us
  other arithmetic: 99.3 us -> 157 us
  Pallas kernels: 103 us -> 60.6 us
  blocking collectives: 0 us -> 28 us
  starting transfers between devices: 163 us -> 136 us
    ppermute x69 -> x53, waiting for transfers between devices: 555 us -> 127 us  [partner(): return lax.ppermute(value, axis, [(i, i ^ bit) for i in range(count)])]
    ppermute x69 -> x53, starting transfers between devices: 139 us -> 63.6 us  [partner(): return lax.ppermute(value, axis, [(i, i ^ bit) for i in range(count)])]
    ppermute x2 -> x34, waiting for transfers between devices: 0.01 us -> 65.7 us  [the longest x4 21 us: gather_z(): lax.ppermute(three, 'z', OUTER)]
    ppermute x2 -> x34, starting transfers between devices: 7.61 us -> 59.1 us  [the longest x4 12.6 us: sum_z(): far, = (yield [lax.ppermute(three.astype(BF16), 'z', INNER)])]
    pallas_call x1, Pallas kernels: 70.6 us -> 30.8 us  [delta_forward(): pl.pallas_call(functools.partial(forward_kernel, heads, rows, size), grid...]
    convert_element_type x6 -> x20, other arithmetic: 5.39 us -> 38.3 us  [the longest x4 7.62 us: sum_z(): (three.astype(F32) + near.astype(F32)).astype(BF16)]
    all_to_all x0 -> x1, blocking collectives: none -> 28 us  [body(): lax.all_to_all(jnp.broadcast_to(after(small, cut)[None], (devices, padded...]
    add x2 -> x4, other arithmetic: 11.8 us -> 24.5 us  [scatter_group(): total = mine.astype(F32) + arrived.astype(F32)]
  transfers between devices with their start and end apart: 75 -> 90, of which waited for: 35 -> 32; matrix products, arithmetic and copies ran while one was open for 19% -> 36% of each run, Pallas kernels for 3% -> 7%
where the time goes in v2:
time: 851 us; the launch traced here: 840 us
  waiting for transfers between devices  208 us (24%)
  other arithmetic  157 us (18%)
  matrix products  156 us (18%)
  starting transfers between devices  136 us (16%)
  local copies, waits for them, and re-layouts  89.1 us (10%)
  Pallas kernels  60.6 us (7%)
  blocking collectives  28 us (3%)
    dot_general x33, matrix products, dot(): lax.dot_general(left, right, (((dim_left,), (dim_right,)), ((), ())), pre...  156 us
    ppermute x53, waiting for transfers between devices, partner(): return lax.ppermute(value, axis, [(i, i ^ bit) for i in range(count)])  127 us
    ppermute x53, starting transfers between devices, partner(): return lax.ppermute(value, axis, [(i, i ^ bit) for i in range(count)])  63.6 us
    unnamed x341, local copies, waits for them, and re-layouts  38.7 us
    pallas_call x1, Pallas kernels, delta_forward(): pl.pallas_call(functools.partial(forward_kernel, heads, rows, size), grid...  30.8 us
    pallas_call x1, Pallas kernels, delta_backward(): pl.pallas_call(functools.partial(backward_kernel, heads, rows, size, step...  29.9 us
    all_to_all x1, blocking collectives, body(): lax.all_to_all(jnp.broadcast_to(after(small, cut)[None], (devices, padded...  28 us
    add x4, other arithmetic, scatter_group(): total = mine.astype(F32) + arrived.astype(F32)  24.5 us
  transfers between devices with their start and end apart: 90, of which 32 were waited for; matrix products, arithmetic and copies ran while one was open for 36% of the time, Pallas kernels for 7%

profile of v2, /device:TPU:0, one launch (start us, length us, event | category | flops | bytes accessed | tf_op | source)
XLA Modules:
  0.0 839.7 jit_solution(11583186170809153408)
XLA Ops:
  13.1 19.0 %collective-permute-done.1 = bf16[1,1,128,2048]{3,2,1,0:T(8,128)(2,1)S(1)} collective-permute-done((bf16[1,1,128,2048]{3,2,1,0:T(8,128)(2,1)S(1)}, bf16[1,1,128,2048]{3,2,1,0:T(8,128)(2,1)S(1)}, u32[]{:S(2)}, u32[]{:S(2)}) %collective-permute-start.1) | collective-permute-done | bytes 524320 | tf_op jit(solution)/shard_map/ppermute | solution.py:436
  48.0 28.0 %all_to_all.28 = bf16[32,2,1024]{2,1,0:T(2,128)(2,1)S(1)} all-to-all(bf16[32,2,1024]{2,1,0:T(2,128)(2,1)S(1)} %reshape.444), channel_id=1, replica_groups=mesh['z'=4,'x'=2,'s'=4] {'z','x','s'}, dimensions={0} | all-to-all | bytes 262144 | tf_op jit(solution)/shard_map/all_to_all | solution.py:637
  86.8 8.9 %collective-permute-done = s32[1,4]{1,0:T(1,128)S(1)} collective-permute-done((s32[1,4]{1,0:T(1,128)S(1)}, s32[1,4]{1,0:T(1,128)S(1)}, u32[]{:S(2)}, u32[]{:S(2)}) %collective-permute-start) | collective-permute-done | bytes 48 | tf_op jit(solution)/shard_map/ppermute | solution.py:436
  149.9 12.1 %collective-permute-done.13 = bf16[512,768]{1,0:T(8,128)(2,1)S(1)} collective-permute-done((bf16[512,768]{1,0:T(8,128)(2,1)}, bf16[512,768]{1,0:T(8,128)(2,1)S(1)}, u32[]{:S(2)}, u32[]{:S(2)}) %collective-permute-start.13) | collective-permute-done | bytes 786464 | tf_op jit(solution)/shard_map/ppermute | solution.py:481
  172.2 12.0 %fusion.181 = f32[2048,896]{1,0:T(8,128)} fusion(bf16[2048,2048]{1,0:T(8,128)(2,1)S(1)} %copy-done.41, bf16[2048,2]{1,0:T(8,128)(2,1)S(1)} %copy.98, bf16[512,768]{1,0:T(8,128)(2,1)S(1)} %add.226, bf16[512,768]{1,0:T(8,128)(2,1)S(1)} %add.225, bf16[512,768]{1,0:T(8,128)(2,1)} %collective-permute-done.5, bf16[512,768]{1,0:T(8,128)(2,1)S(1)} %bitcast.269), kind=kOutput, calls=%fused_computation.393 | convolution fusion | flops 7538212864 | bytes 18882560 | tf_op jit(solution)/shard_map/dot_general | solution.py:586
  188.1 30.8 %delta_forward.1 = (bf16[2,2,2,2,128,256]{5,4,3,2,1,0:T(8,128)(2,1)S(1)}, f32[2,2,2,2,128,256]{5,4,3,2,1,0:T(8,128)S(1)}, bf16[8,4,128,128]{3,2,1,0:T(8,128)(2,1...) custom-call(s32[2,4]{1,0:T(2,128)S(1)} %pad_add_fusion.starts, ...), custom_call_target="tpu_custom_call" | custom-call | flops 40265318400 | bytes 14680064 | tf_op jit(solution)/shard_map/delta_forward/pallas_call | solution.py:325
  251.0 10.5 %collective-permute-done.29 = bf16[2,512,704]{1,2,0:T(8,128)(2,1)} collective-permute-done((bf16[2,512,704]{1,2,0:T(8,128)(2,1)S(1)}, bf16[2,512,704]{1,2,0:T(8,128)(2,1)}, u32[]{:S(2)}, u32[]{:S(2)}) %collective-permute-start.29) | collective-permute-done | bytes 1441824 | tf_op jit(solution)/shard_map/ppermute | solution.py:480
  261.5 12.2 %collective-permute-done.27 = bf16[2,1,128,2048]{3,2,1,0:T(8,128)(2,1)S(1)} collective-permute-done((bf16[2,1,128,2048]{3,2,1,0:T(8,128)(2,1)S(1)}, bf16[2,1,128,2048]{3,2,1,0:T(8,128)(2,1)S(1)}, u32[]{:S(2)}, u32[]{:S(2)}) %collective-permute-start.27) | collective-permute-done | bytes 1048608 | tf_op jit(solution)/shard_map/ppermute | solution.py:436
  300.1 9.7 %collective-permute-done.33 = bf16[1,1,128,2048]{3,2,1,0:T(8,128)(2,1)S(1)} collective-permute-done((bf16[1,1,128,2048]{3,2,1,0:T(8,128)(2,1)S(1)}, bf16[1,1,128,2048]{3,2,1,0:T(8,128)(2,1)S(1)}, u32[]{:S(2)}, u32[]{:S(2)}) %collective-permute-start.33) | collective-permute-done | bytes 524320 | tf_op jit(solution)/shard_map/ppermute | solution.py:436
  320.8 14.4 %collective-permute-done.38 = bf16[704,512]{1,0:T(8,128)(2,1)S(1)} collective-permute-done((bf16[704,512]{1,0:T(8,128)(2,1)S(1)}, bf16[704,512]{1,0:T(8,128)(2,1)S(1)}, u32[]{:S(2)}, u32[]{:S(2)}) %collective-permute-start.38) | collective-permute-done | bytes 720928 | tf_op jit(solution)/shard_map/ppermute | solution.py:436
  371.0 8.1 fusion.9
  379.2 7.9 fusion.8
  391.3 16.2 %multiply_convert_fusion = (bf16[2048,704]{0,1:T(8,128)(2,1)}, bf16[2048,704]{0,1:T(8,128)(2,1)}, bf16[2048,704]{0,1:T(8,128)(2,1)}) fusion(f32[2048,704]{0,1:T(8,128)} %fusion.8, f32[2048,704]{0,1:T(8,128)} %fusion.9, bf16[2048,2048]{1,0:T(8,128)(2,1)} %bitcast.245, bf16[704,512]{1,0:T(8,128)(2,1)} %add.245, bf16[704,512]{1,0:T(8,128)(2,1)} %add.244, ...), kind=kOutput, calls=%fused_computation.16 | convolution fusion | flops 5940183040 | bytes 31457280 | tf_op jit(solution)/shard_map/dot_general | solution.py:586
  407.5 9.3 %fusion.7 = f32[1024,2048]{1,0:T(8,128)} fusion(bf16[2,2048,704]{1,2,0:T(8,128)(2,1)} %copy-done.50, bf16[2048,704]{0,1:T(8,128)(2,1)} %get-tuple-element.356), kind=kOutput, calls=%fused_computation.66 | convolution fusion | flops 2952790016 | bytes 12713984 | tf_op jit(solution)/shard_map/dot_general | solution.py:586
  416.7 8.3 add_convert_fusion
  478.2 13.8 %collective-permute-done.45 = bf16[2,1,128,2048]{3,2,1,0:T(8,128)(2,1)S(1)} collective-permute-done((bf16[2,1,128,2048]{3,2,1,0:T(8,128)(2,1)S(1)}, bf16[2,1,128,2048]{3,2,1,0:T(8,128)(2,1)S(1)}, u32[]{:S(2)}, u32[]{:S(2)}) %collective-permute-start.45) | collective-permute-done | bytes 1048608 | tf_op jit(solution)/shard_map/ppermute | solution.py:436
  537.9 18.5 %collective-permute-done.57 = bf16[2,512,704]{1,2,0:T(8,128)(2,1)S(1)} collective-permute-done((bf16[2,512,704]{1,2,0:T(8,128)(2,1)S(1)}, bf16[2,512,704]{1,2,0:T(8,128)(2,1)S(1)}, u32[]{:S(2)}, u32[]{:S(2)}) %collective-permute-start.57) | collective-permute-done | bytes 1441824 | tf_op jit(solution)/shard_map/ppermute | solution.py:493
  612.4 29.9 %delta_backward.1 = (bf16[2,2,2,2,128,896]{5,4,3,2,1,0:T(8,128)(2,1)}, f32[4,768]{1,0:T(4,128)S(1)}, f32[1,256]{1,0:T(1,128)S(1)}) custom-call(s32[2,4]{1,0:T(2,128)S(1)} %pad_add_fusion.starts, s32[1]{0:T(128)} %bitcast.2.place, f32[2,2,2,2,128,896]{5,4,3,2,1,0:T(8,128)} %bitcast.285, f32[2,2,2,2,128,896]{5,4,3,2,1,0:T(8,128)} %bitcast.286, ...), custom_call_target="tpu_custom_call" | custom-call | flops 46976204800 | bytes 18350080 | tf_op jit(solution)/shard_map/delta_backward/pallas_call | solution.py:391
  679.3 9.1 %convolution_convert_fusion.2 = bf16[1024,2048]{1,0:T(8,128)(2,1)} fusion(bf16[2048,896]{1,0:T(8,128)(2,1)S(1)} %bitcast.290, bf16[2048,2]{1,0:T(8,128)(2,1)S(1)} %copy-done.119, bf16[512,768]{1,0:T(8,128)(2,1)S(1)} %copy-done.98, bf16[512,768]{1,0:T(8,128)(2,1)S(1)} %copy-done.96, bf16[512,768]{1,0:T(8,128)(2,1)} %collective-permute-done.5, ...), kind=kOutput, calls=%fused_computation.31 | convolution fusion | flops 3782213632 | bytes 9699328 | tf_op jit(solution)/shard_map/dot_general | solution.py:586
  693.8 9.0 %fusion.59 = f32[1024,2048]{1,0:T(8,128)} fusion(bf16[2048,896]{1,0:T(8,128)(2,1)S(1)} %bitcast.293, bf16[2048,2]{1,0:T(8,128)(2,1)S(1)} %copy-done.119, bf16[512,768]{1,0:T(8,128)(2,1)S(1)} %copy-done.98, bf16[512,768]{1,0:T(8,128)(2,1)S(1)} %copy-done.96, bf16[512,768]{1,0:T(8,128)(2,1)} %collective-permute-done.5, bf16[512,768]{1,0:T(8,128)(2,1)S(1)} %bitcast.271), kind=kOutput, calls=%fused_computation.150 | convolution fusion | flops 3780116480 | bytes 13893632 | tf_op jit(solution)/shard_map/dot_general | solution.py:586
  721.6 7.9 all-to-all-done.3
  768.1 9.2 %collective-permute-done.74 = bf16[2,1,128,2048]{3,2,1,0:T(8,128)(2,1)S(1)} collective-permute-done((bf16[2,1,128,2048]{3,2,1,0:T(8,128)(2,1)}, bf16[2,1,128,2048]{3,2,1,0:T(8,128)(2,1)S(1)}, u32[]{:S(2)}, u32[]{:S(2)}) %collective-permute-start.74) | collective-permute-done | bytes 1048608 | tf_op jit(solution)/shard_map/ppermute | solution.py:436
  788.6 9.3 %collective-permute-done.80 = bf16[1,1,128,2048]{3,2,1,0:T(8,128)(2,1)S(1)} collective-permute-done((bf16[1,1,128,2048]{3,2,1,0:T(8,128)(2,1)}, bf16[1,1,128,2048]{3,2,1,0:T(8,128)(2,1)S(1)}, u32[]{:S(2)}, u32[]{:S(2)}) %collective-permute-start.80) | collective-permute-done | bytes 524320 | tf_op jit(solution)/shard_map/ppermute | solution.py:436
  826.0 8.2 all-to-all-done.2
  (733 shorter events, 513.6 us)
Async XLA Ops:
  33.3 43.5 %collective-permute-start.4 = (bf16[1,2,128,2048]{3,2,1,0:T(8,128)(2,1)}, bf16[1,2,128,2048]{3,2,1,0:T(8,128)(2,1)}, u32[]{:S(2)}, u32[]{:S(2)}) collective-permute-start(bf16[1,2,128,2048]{3,2,1,0:T(8,128)(2,1)} %pad_maximum_fusion.16), channel_id=1, source_target_pairs={{0,4},{4,0},{1,5},{5,1},{2,6},{6,2},{3,7},{7,3},{8,12},{12,8},{9,1... | collective-permute-start | bytes 3145736 | tf_op jit(solution)/shard_map/ppermute | solution.py:436
  35.8 41.0 %collective-permute-start.3 = (bf16[2,1,128,2048]{3,2,1,0:T(8,128)(2,1)}, bf16[2,1,128,2048]{3,2,1,0:T(8,128)(2,1)}, u32[]{:S(2)}, u32[]{:S(2)}) collective-permute-start(bf16[2,1,128,2048]{3,2,1,0:T(8,128)(2,1)} %pad_maximum_fusion.15), channel_id=1, source_target_pairs={{0,2},{1,3},{2,0},{3,1},{4,6},{5,7},{6,4},{7,5},{8,10},{9,11},{10,... | collective-permute-start | bytes 3145736 | tf_op jit(solution)/shard_map/ppermute | solution.py:436
  40.1 36.7 %collective-permute-start.5 = (bf16[512,768]{1,0:T(8,128)(2,1)}, bf16[512,768]{1,0:T(8,128)(2,1)}, u32[]{:S(2)}, u32[]{:S(2)}) collective-permute-start(bf16[512,768]{1,0:T(8,128)(2,1)} %bitcast.267), channel_id=1, source_target_pairs={{0,8},{8,0},{16,24},{24,16},{1,9},{9,1},{17,25},{25,17},{2,10},{10... | collective-permute-start | bytes 2359304 | tf_op jit(solution)/shard_map/ppermute | solution.py:436
  42.6 35.1 %collective-permute-start.7 = (bf16[2,256,704]{1,2,0:T(8,128)(2,1)S(1)}, bf16[2,256,704]{1,2,0:T(8,128)(2,1)}, u32[]{:S(2)}, u32[]{:S(2)}) collective-permute-start(bf16[2,256,704]{1,2,0:T(8,128)(2,1)S(1)} %broadcast_select_fusion.3), channel_id=1, source_target_pairs={{0,4},{4,0},{1,5},{5,1},{2,6},{6,2},{3,7},{7,3},{8,12},{12,8},{9,1... | collective-permute-start | bytes 2162696 | tf_op jit(solution)/shard_map/ppermute | solution.py:436
  83.9 43.1 %collective-permute-start.8 = (bf16[2,2,2,128,2048]{4,3,2,1,0:T(8,128)(2,1)}, bf16[2,2,2,128,2048]{4,3,2,1,0:T(8,128)(2,1)}, u32[]{:S(2)}, u32[]{:S(2)}) collective-permute-start(bf16[2,2,2,128,2048]{4,3,2,1,0:T(8,128)(2,1)} %pad_maximum_fusion.4), channel_id=1, source_target_pairs={{0,1},{1,0},{2,3},{3,2},{4,5},{5,4},{6,7},{7,6},{8,9},{9,8},{10,11... | collective-permute-start | bytes 12582920 | tf_op jit(solution)/shard_map/ppermute | solution.py:436
  84.6 42.3 %collective-permute-start.11 = (bf16[704,256]{1,0:T(8,128)(2,1)}, bf16[704,256]{1,0:T(8,128)(2,1)}, u32[]{:S(2)}, u32[]{:S(2)}) collective-permute-start(bf16[704,256]{1,0:T(8,128)(2,1)} %broadcast_select_fusion.7), channel_id=1, source_target_pairs={{0,4},{4,0},{1,5},{5,1},{2,6},{6,2},{3,7},{7,3},{8,12},{12,8},{9,1... | collective-permute-start | bytes 1081352 | tf_op jit(solution)/shard_map/ppermute | solution.py:436
  166.3 52.6 %collective-permute-start.20 = (bf16[2,512,704]{1,2,0:T(8,128)(2,1)}, bf16[2,512,704]{1,2,0:T(8,128)(2,1)}, u32[]{:S(2)}, u32[]{:S(2)}) collective-permute-start(bf16[2,512,704]{1,2,0:T(8,128)(2,1)} %pad_maximum_fusion.10), channel_id=1, source_target_pairs={{0,8},{8,0},{16,24},{24,16},{1,9},{9,1},{17,25},{25,17},{2,10},{10... | collective-permute-start | bytes 4325384 | tf_op jit(solution)/shard_map/ppermute | solution.py:436
  186.4 35.0 %collective-permute-start.24 = (bf16[1,2,128,2048]{3,2,1,0:T(8,128)(2,1)S(1)}, bf16[1,2,128,2048]{3,2,1,0:T(8,128)(2,1)S(1)}, u32[]{:S(2)}, u32[]{:S(2)}) collective-permute-start(bf16[1,2,128,2048]{3,2,1,0:T(8,128)(2,1)S(1)} %pad_maximum_fusion.19), channel_id=1, source_target_pairs={{0,4},{4,0},{1,5},{5,1},{2,6},{6,2},{3,7},{7,3},{8,12},{12,8},{9,1... | collective-permute-start | bytes 3145736 | tf_op jit(solution)/shard_map/ppermute | solution.py:436
  225.7 35.8 %collective-permute-start.29 = (bf16[2,512,704]{1,2,0:T(8,128)(2,1)S(1)}, bf16[2,512,704]{1,2,0:T(8,128)(2,1)}, u32[]{:S(2)}, u32[]{:S(2)}) collective-permute-start(bf16[2,512,704]{1,2,0:T(8,128)(2,1)S(1)} %collective-permute-done.21), channel_id=1, source_target_pairs={{8,0},{16,24},{9,1},{17,25},{10,2},{18,26},{11,3},{19,27},{12,4},{... | collective-permute-start | bytes 4325384 | tf_op jit(solution)/shard_map/ppermute | solution.py:480
  432.7 45.5 %collective-permute-start.47 = (bf16[704,512]{1,0:T(8,128)(2,1)}, bf16[704,512]{1,0:T(8,128)(2,1)}, u32[]{:S(2)}, u32[]{:S(2)}) collective-permute-start(bf16[704,512]{1,0:T(8,128)(2,1)} %fusion.112), channel_id=1, source_target_pairs={{0,8},{24,16},{1,9},{25,17},{2,10},{26,18},{3,11},{27,19},{4,12},{... | collective-permute-start | bytes 2162696 | tf_op jit(solution)/shard_map/ppermute | solution.py:491
  499.3 57.1 %collective-permute-start.59 = (bf16[2,2,2,128,2048]{4,3,2,1,0:T(8,128)(2,1)}, bf16[2,2,2,128,2048]{4,3,2,1,0:T(8,128)(2,1)S(1)}, u32[]{:S(2)}, u32[]{:S(2)}) collective-permute-start(bf16[2,2,2,128,2048]{4,3,2,1,0:T(8,128)(2,1)} %bitcast.57), channel_id=1, source_target_pairs={{0,1},{1,0},{2,3},{3,2},{4,5},{5,4},{6,7},{7,6},{8,9},{9,8},{10,11... | collective-permute-start | bytes 12582920 | tf_op jit(solution)/shard_map/ppermute | solution.py:436
  562.3 37.4 %collective-permute-start.60 = (bf16[2,2,2,128,2048]{4,3,2,1,0:T(8,128)(2,1)}, bf16[2,2,2,128,2048]{4,3,2,1,0:T(8,128)(2,1)}, u32[]{:S(2)}, u32[]{:S(2)}) collective-permute-start(bf16[2,2,2,128,2048]{4,3,2,1,0:T(8,128)(2,1)} %pad_maximum_fusion.7), channel_id=1, source_target_pairs={{0,1},{1,0},{2,3},{3,2},{4,5},{5,4},{6,7},{7,6},{8,9},{9,8},{10,11... | collective-permute-start | bytes 12582920 | tf_op jit(solution)/shard_map/ppermute | solution.py:436
  572.1 35.6 %collective-permute-start.62 = (bf16[704,512]{1,0:T(8,128)(2,1)}, bf16[704,512]{1,0:T(8,128)(2,1)}, u32[]{:S(2)}, u32[]{:S(2)}) collective-permute-start(bf16[704,512]{1,0:T(8,128)(2,1)} %add_convert_fusion.8), channel_id=1, source_target_pairs={{8,16},{16,8},{9,17},{17,9},{10,18},{18,10},{11,19},{19,11},{12,20... | collective-permute-start | bytes 2162696 | tf_op jit(solution)/shard_map/ppermute | solution.py:498
  582.9 61.8 %collective-permute-start.64 = (bf16[2,512,704]{1,2,0:T(8,128)(2,1)}, bf16[2,512,704]{1,2,0:T(8,128)(2,1)}, u32[]{:S(2)}, u32[]{:S(2)}) collective-permute-start(bf16[2,512,704]{1,2,0:T(8,128)(2,1)} %add_convert_fusion.1), channel_id=1, source_target_pairs={{8,16},{16,8},{9,17},{17,9},{10,18},{18,10},{11,19},{19,11},{12,20... | collective-permute-start | bytes 4325384 | tf_op jit(solution)/shard_map/ppermute | solution.py:498
  586.3 61.2 %collective-permute-start.63 = (bf16[2,512,704]{1,2,0:T(8,128)(2,1)}, bf16[2,512,704]{1,2,0:T(8,128)(2,1)}, u32[]{:S(2)}, u32[]{:S(2)}) collective-permute-start(bf16[2,512,704]{1,2,0:T(8,128)(2,1)} %add_convert_fusion.2), channel_id=1, source_target_pairs={{0,8},{8,0},{16,24},{24,16},{1,9},{9,1},{17,25},{25,17},{2,10},{10... | collective-permute-start | bytes 4325384 | tf_op jit(solution)/shard_map/ppermute | solution.py:436
  599.8 54.8 %collective-permute-start.66 = (bf16[2,1,128,2048]{3,2,1,0:T(8,128)(2,1)}, bf16[2,1,128,2048]{3,2,1,0:T(8,128)(2,1)}, u32[]{:S(2)}, u32[]{:S(2)}) collective-permute-start(bf16[2,1,128,2048]{3,2,1,0:T(8,128)(2,1)} %slice.1093), channel_id=1, source_target_pairs={{0,2},{1,3},{2,0},{3,1},{4,6},{5,7},{6,4},{7,5},{8,10},{9,11},{10,... | collective-permute-start | bytes 3145736 | tf_op jit(solution)/shard_map/ppermute | solution.py:436
  607.7 46.9 %collective-permute-start.67 = (bf16[1,2,128,2048]{3,2,1,0:T(8,128)(2,1)}, bf16[1,2,128,2048]{3,2,1,0:T(8,128)(2,1)}, u32[]{:S(2)}, u32[]{:S(2)}) collective-permute-start(bf16[1,2,128,2048]{3,2,1,0:T(8,128)(2,1)} %fusion.150), channel_id=1, source_target_pairs={{0,4},{4,0},{1,5},{5,1},{2,6},{6,2},{3,7},{7,3},{8,12},{12,8},{9,1... | collective-permute-start | bytes 3145736 | tf_op jit(solution)/shard_map/ppermute | solution.py:436
  610.6 56.3 %collective-permute-start.68 = (bf16[704,256]{1,0:T(8,128)(2,1)}, bf16[704,256]{1,0:T(8,128)(2,1)S(1)}, u32[]{:S(2)}, u32[]{:S(2)}) collective-permute-start(bf16[704,256]{1,0:T(8,128)(2,1)} %select_convert_fusion.1), channel_id=1, source_target_pairs={{0,4},{4,0},{1,5},{5,1},{2,6},{6,2},{3,7},{7,3},{8,12},{12,8},{9,1... | collective-permute-start | bytes 1081352 | tf_op jit(solution)/shard_map/ppermute | solution.py:436
  651.0 90.7 %collective-permute-start.73 = (bf16[2,256,704]{1,2,0:T(8,128)(2,1)}, bf16[2,256,704]{1,2,0:T(8,128)(2,1)}, u32[]{:S(2)}, u32[]{:S(2)}) collective-permute-start(bf16[2,256,704]{1,2,0:T(8,128)(2,1)} %select_convert_fusion), channel_id=1, source_target_pairs={{0,4},{4,0},{1,5},{5,1},{2,6},{6,2},{3,7},{7,3},{8,12},{12,8},{9,1... | collective-permute-start | bytes 2162696 | tf_op jit(solution)/shard_map/ppermute | solution.py:436
  655.6 79.4 %collective-permute-start.70 = (bf16[64,2048]{1,0:T(8,128)(2,1)}, bf16[64,2048]{1,0:T(8,128)(2,1)}, u32[]{:S(2)}, u32[]{:S(2)}) collective-permute-start(bf16[64,2048]{1,0:T(8,128)(2,1)} %get-tuple-element.343), channel_id=1, source_target_pairs={{0,8},{24,16},{1,9},{25,17},{2,10},{26,18},{3,11},{27,19},{4,12},{... | collective-permute-start | bytes 786440 | tf_op jit(solution)/shard_map/ppermute | solution.py:493
  657.6 77.4 %collective-permute-start.71 = (bf16[64,2048]{1,0:T(8,128)(2,1)}, bf16[64,2048]{1,0:T(8,128)(2,1)}, u32[]{:S(2)}, u32[]{:S(2)}) collective-permute-start(bf16[64,2048]{1,0:T(8,128)(2,1)} %get-tuple-element.342), channel_id=1, source_target_pairs={{8,16},{16,8},{9,17},{17,9},{10,18},{18,10},{11,19},{19,11},{12,20... | collective-permute-start | bytes 786440 | tf_op jit(solution)/shard_map/ppermute | solution.py:494
  671.4 59.9 %collective-permute-start.69 = (bf16[512,768]{1,0:T(8,128)(2,1)}, bf16[512,768]{1,0:T(8,128)(2,1)}, u32[]{:S(2)}, u32[]{:S(2)}) collective-permute-start(bf16[512,768]{1,0:T(8,128)(2,1)} %fusion.68), channel_id=1, source_target_pairs={{0,8},{24,16},{1,9},{25,17},{2,10},{26,18},{3,11},{27,19},{4,12},{... | collective-permute-start | bytes 2359304 | tf_op jit(solution)/shard_map/ppermute | solution.py:491
  688.3 53.4 %collective-permute-start.72 = (bf16[2,2,2,128,2048]{4,3,2,1,0:T(8,128)(2,1)}, bf16[2,2,2,128,2048]{4,3,2,1,0:T(8,128)(2,1)}, u32[]{:S(2)}, u32[]{:S(2)}) collective-permute-start(bf16[2,2,2,128,2048]{4,3,2,1,0:T(8,128)(2,1)} %bitcast.68), channel_id=1, source_target_pairs={{0,1},{1,0},{2,3},{3,2},{4,5},{5,4},{6,7},{7,6},{8,9},{9,8},{10,11... | collective-permute-start | bytes 12582920 | tf_op jit(solution)/shard_map/ppermute | solution.py:436
  736.8 42.5 %collective-permute-start.79 = (bf16[64,2048]{1,0:T(8,128)(2,1)}, bf16[64,2048]{1,0:T(8,128)(2,1)S(1)}, u32[]{:S(2)}, u32[]{:S(2)}) collective-permute-start(bf16[64,2048]{1,0:T(8,128)(2,1)} %add_convert_fusion.12), channel_id=1, source_target_pairs={{8,16},{16,8},{9,17},{17,9},{10,18},{18,10},{11,19},{19,11},{12,20... | collective-permute-start | bytes 786440 | tf_op jit(solution)/shard_map/ppermute | solution.py:498
  (231 other events, 2797.9 us)
